TPU v7x, 32 devices: a whole 2x2x4 slice. The times are simulated.
32 devices in a mesh: dp: 16 (over z, x, core), mp: 2 (over y).
Axes of the slice: x: 2, y: 2, z: 4, core: 2. Of those that a mesh axis runs over, the one named last changes fastest.
Arguments:
- corpus: bfloat16 [2048, 16, 320], P('dp'), may hold values from -6 to 6
- picks: int32 [16, 16], P('dp'), may hold values from 0 to 127
- lengths: int32 [2048], P('dp'), may hold values from 1 to 16, 24576 in all
- langs: int32 [2048], P('dp'), may hold values from 0 to 127
- w_in: bfloat16 [320, 1536], P(None, 'mp'), may hold values from -0.3125 to 0.3125
- lang_table: bfloat16 [128, 1536], P(None, 'mp'), may hold values from -3 to 3
- ln_gain: float32 [1536], P('mp'), may hold values from 0.1 to 1.9
- w_pw1: bfloat16 [1536, 2, 1536], P('dp', None, 'mp'), may hold values from -0.15625 to 0.15625
- kernel: float32 [31, 1536], P(None, 'mp'), may hold values from -1.5 to 1.5
- bn_gain: float32 [1536], P('mp'), may hold values from 0.1 to 1.9
- bn_bias: float32 [1536], P('mp'), may hold values from -3 to 3
- w_pw2: bfloat16 [1536, 1536], P('dp', 'mp'), may hold values from -0.15625 to 0.15625
- cotangent: bfloat16 [4096, 1536], P('dp', 'mp'), may hold values from -6 to 6
Outputs:
- encoded: bfloat16 [4096, 1536], P('dp', 'mp')
- grad_pw1: float32 [1536, 2, 1536], P('dp', None, 'mp')
- grad_pw2: float32 [1536, 1536], P('dp', 'mp')
- grad_kernel: float32 [31, 1536], P(None, 'mp')
- grad_bn_gain: float32 [1536], P('mp')
- grad_bn_bias: float32 [1536], P('mp')
Inputs may be any that keep to these rules, and one draw needn't show every extreme that they name: `picks`: each trainer takes one block of every shard; a shard may give the same block to several trainers.
All inputs are finite; a program needn't handle non-finite values. No bound on the sum of `lengths` on one device may be relied on, other than what follows from the above.
Results may differ from a plain program's by a relative error of at most 0.0057.
Values may be sent and summed in bfloat16 or wider, within the bound.
A program may use at most 64 MiB of HBM per device.

v0:
```python
import jax
import jax.numpy as jnp
from jax import lax
from jax.sharding import PartitionSpec as P

EPS = 1e-05


def depth_conv(values, taps, frames):
    chans = values.shape[1]
    shaped = values.reshape(-1, frames, chans)
    margin = taps.shape[0] // 2
    padded = jnp.pad(shaped, ((0, 0), (margin, margin), (0, 0)))
    total = jnp.zeros(shaped.shape, jnp.float32)
    for step in range(taps.shape[0]):
        total = total + taps[step] * padded[:, step : step + frames]
    return total.reshape(values.shape)


def depth_back(grads, taps, frames):
    chans = grads.shape[1]
    shaped = grads.reshape(-1, frames, chans)
    margin = taps.shape[0] // 2
    padded = jnp.pad(shaped, ((0, 0), (margin, margin), (0, 0)))
    total = jnp.zeros(shaped.shape, jnp.float32)
    for step in range(taps.shape[0]):
        begin = 2 * margin - step
        total = total + taps[step] * padded[:, begin : begin + frames]
    return total.reshape(grads.shape)


def kernel_terms(grads, values, width, frames):
    chans = values.shape[1]
    shaped = values.reshape(-1, frames, chans)
    grad_shaped = grads.reshape(-1, frames, chans)
    margin = width // 2
    padded = jnp.pad(shaped, ((0, 0), (margin, margin), (0, 0)))
    rows_out = []
    for step in range(width):
        rows_out.append(jnp.sum(grad_shaped * padded[:, step : step + frames], axis=(0, 1)))
    return jnp.stack(rows_out, 0)


def contract_rows(left, right):
    return lax.dot_general(
        left, right, (((0,), (0,)), ((), ())), preferred_element_type=jnp.float32
    )


def on_device(
    corpus,
    picks,
    lengths,
    langs,
    w_in,
    lang_table,
    ln_gain,
    w_pw1,
    kernel,
    bn_gain,
    bn_bias,
    w_pw2,
    cotangent,
):
    model_width = w_pw2.shape[0] * lax.axis_size("dp")
    chosen = picks[0]
    blocks = jnp.take(corpus, chosen, axis=0)
    lens_send = jnp.take(lengths, chosen)
    lang_send = jnp.take(langs, chosen)
    received, lens, lang = (
        lax.all_to_all(blocks, "dp", split_axis=0, concat_axis=0, tiled=True),
        lax.all_to_all(lens_send, "dp", split_axis=0, concat_axis=0, tiled=True),
        lax.all_to_all(lang_send, "dp", split_axis=0, concat_axis=0, tiled=True),
    )
    frames = received.shape[1]
    valid = (
        (jnp.arange(frames, dtype=jnp.int32)[None, :] < lens[:, None])
        .astype(jnp.float32)
        .reshape(-1)
    )
    valid_col = valid[:, None]
    mel = received.reshape(-1, received.shape[2]) * valid_col.astype(jnp.bfloat16)
    onehot = (lang[:, None] == jnp.arange(lang_table.shape[0], dtype=jnp.int32)[None, :]).astype(
        jnp.bfloat16
    )
    lang_rows = jnp.dot(onehot, lang_table, preferred_element_type=jnp.float32)
    inputs = jnp.dot(mel, w_in, preferred_element_type=jnp.float32) + jnp.repeat(
        lang_rows, frames, axis=0
    )
    row_sum, row_sq = lax.psum((jnp.sum(inputs, 1), jnp.sum(inputs * inputs, 1)), "mp")
    mean = row_sum / model_width
    var = row_sq / model_width - mean * mean
    normed_in = ((inputs - mean[:, None]) * lax.rsqrt(var + EPS)[:, None] * ln_gain).astype(
        jnp.bfloat16
    )
    weights_one = lax.all_gather(w_pw1, "dp", axis=0, tiled=True).reshape(model_width, -1)
    half = weights_one.shape[1] // 2
    normed_full = lax.all_gather(normed_in, "mp", axis=1, tiled=True)
    pre = jnp.dot(normed_full, weights_one, preferred_element_type=jnp.float32)
    linear_part = pre[:, :half]
    gate_part = pre[:, half:]
    gate_sig = jax.nn.sigmoid(gate_part)
    glu_out = linear_part * gate_sig * valid_col
    conv_out = depth_conv(glu_out, kernel, frames)
    sum_conv, sum_sq, count = lax.psum(
        (
            jnp.sum(valid_col * conv_out, 0),
            jnp.sum(valid_col * conv_out * conv_out, 0),
            jnp.sum(valid),
        ),
        "dp",
    )
    mu_conv = sum_conv / count
    var_conv = sum_sq / count - mu_conv * mu_conv
    inv_std = lax.rsqrt(var_conv + EPS)
    normed_conv = (conv_out - mu_conv) * inv_std
    act = normed_conv * bn_gain + bn_bias
    act_sig = jax.nn.sigmoid(act)
    hidden = (valid_col * act * act_sig).astype(jnp.bfloat16)
    weights_two = lax.all_gather(w_pw2, "dp", axis=0, tiled=True)
    hidden_full = lax.all_gather(hidden, "mp", axis=1, tiled=True)
    encoded = (
        inputs + jnp.dot(hidden_full, weights_two, preferred_element_type=jnp.float32)
    ).astype(jnp.bfloat16)
    grad_pw2 = lax.psum_scatter(
        contract_rows(hidden_full, cotangent), "dp", scatter_dimension=0, tiled=True
    )
    cot_full = lax.all_gather(cotangent, "mp", axis=1, tiled=True)
    weights_rows = lax.all_to_all(weights_two, "mp", split_axis=0, concat_axis=1, tiled=True)
    dhidden = lax.dot_general(
        cot_full, weights_rows, (((1,), (1,)), ((), ())), preferred_element_type=jnp.float32
    )
    dact = dhidden * valid_col * act_sig * (1.0 + act * (1.0 - act_sig))
    grad_bias, grad_gain = lax.psum((jnp.sum(dact, 0), jnp.sum(dact * normed_conv, 0)), "dp")
    dconv = (
        valid_col * inv_std * bn_gain * (dact - grad_bias / count - normed_conv * grad_gain / count)
    )
    grad_kernel = lax.psum(kernel_terms(dconv, glu_out, kernel.shape[0], frames), "dp")
    dglu = depth_back(dconv, kernel, frames)
    dlin = dglu * valid_col * gate_sig
    dgate = dglu * valid_col * linear_part * gate_sig * (1.0 - gate_sig)
    dpre = jnp.concatenate([dlin, dgate], 1).astype(jnp.bfloat16)
    grad_pw1 = lax.psum_scatter(
        contract_rows(normed_full, dpre), "dp", scatter_dimension=0, tiled=True
    )
    grad_pw1 = grad_pw1.reshape(grad_pw1.shape[0], 2, half)
    return (encoded, grad_pw1, grad_pw2, grad_kernel, grad_gain, grad_bias)


def solution(mesh):
    return jax.shard_map(
        on_device,
        mesh=mesh,
        in_specs=(
            P("dp", None, None),
            P("dp", None),
            P("dp"),
            P("dp"),
            P(None, "mp"),
            P(None, "mp"),
            P("mp"),
            P("dp", None, "mp"),
            P(None, "mp"),
            P("mp"),
            P("mp"),
            P("dp", "mp"),
            P("dp", "mp"),
        ),
        out_specs=(
            P("dp", "mp"),
            P("dp", None, "mp"),
            P("dp", "mp"),
            P(None, "mp"),
            P("mp"),
            P("mp"),
        ),
        check_vma=False,
    )
```

profile of v0, /device:TPU:8, one launch (start us, length us, event | category | flops | bytes accessed | tf_op | source)
XLA Modules:
  0.0 484.4 jit_solution(15483893597884759426)
XLA Ops:
  7.2 0.7 all-gather.5.cloned.1.call-update
  8.0 0.7 all-gather.3.cloned.1.call-update
  8.7 0.7 compare_select_fusion.1
  9.4 1.3 gather_fusion.1
  10.7 0.7 select_bitcast_fusion.1
  11.3 0.7 copy.27
  12.0 6.3 %all-to-all-start.1 = ((s32[16,1,1]{2,1,0:T(1,128)}), s32[16,1,1]{2,1,0:T(1,128)S(1)}, u32[]{:S(2)}, u32[]{:S(2)}) async-start(s32[16,1,1]{2,1,0:T(1,128)} %copy.27), calls=%async_computation.1 | async-start | bytes 16384 | tf_op jit(solution)/shard_map/all_to_all | solution.py:72
  18.3 1.3 gather_fusion.2
  19.6 2.2 copy.26
  21.9 0.6 gather_fusion
  22.5 0.8 slice_reduce_fusion.30
  23.2 11.9 %all_gather.19 = bf16[256,1536]{1,0:T(8,128)(2,1)} all-gather(bf16[256,768]{1,0:T(8,128)(2,1)S(1)} %copy-done.7), channel_id=1, replica_groups=mesh['dp'=16,'mp'=2] {'mp'}, dimensions={1}, use_global_device_ids=true | all-gather | bytes 1179648 | tf_op jit(solution)/shard_map/all_gather | solution.py:128
  35.2 0.8 broadcast_select_fusion
  35.9 0.7 slice_reduce_fusion.29
  36.6 0.7 copy.28
  37.3 6.0 %all-to-all-start.2 = ((s32[16,1,1]{2,1,0:T(1,128)}), s32[16,1,1]{2,1,0:T(1,128)S(1)}, u32[]{:S(2)}, u32[]{:S(2)}) async-start(s32[16,1,1]{2,1,0:T(1,128)} %copy.28), calls=%async_computation.2 | async-start | bytes 16384 | tf_op jit(solution)/shard_map/all_to_all | solution.py:73
  43.3 0.4 reduce.4
  43.7 0.1 fusion.72
  43.8 0.1 reshape.177
  43.9 0.6 convert_element_type.44
  44.4 3.8 all-to-all-done.2
  48.2 4.9 %all-to-all-start = ((bf16[16,16,320]{2,1,0:T(8,128)(2,1)}), bf16[16,16,320]{2,1,0:T(8,128)(2,1)S(1)}, u32[]{:S(2)}, u32[]{:S(2)}) async-start(bf16[16,16,320]{2,1,0:T(8,128)(2,1)} %broadcast_select_fusion), calls=%async_computation | async-start | bytes 393216 | tf_op jit(solution)/shard_map/all_to_all | solution.py:71
  53.1 0.4 reduce.5
  53.5 0.7 fusion.75
  54.2 0.2 fusion.73
  54.4 4.9 %all-to-all-done = bf16[16,16,320]{2,1,0:T(8,128)(2,1)S(1)} async-done(((bf16[16,16,320]{2,1,0:T(8,128)(2,1)}), bf16[16,16,320]{2,1,0:T(8,128)(2,1)S(1)}, u32[]{:S(2)}, u32[]{:S(2)}) %all-to-all-start) | async-done | bytes 163872 | tf_op jit(solution)/shard_map/all_to_all | solution.py:71
  59.3 3.8 all-to-all-start.3
  63.1 0.0 reduce-scatter.3.cloned.1.call-start
  63.2 0.8 bitcast_multiply_fusion.1
  63.9 0.1 broadcast_in_dim.17
  64.0 1.3 fusion.79
  65.3 26.7 %all-reduce.4 = (f32[256]{0:T(256)S(1)}, f32[256]{0:T(256)S(1)}) all-reduce(f32[256]{0:T(256)S(1)} %get-tuple-element.42, f32[256]{0:T(256)S(1)} %get-tuple-element.41), channel_id=1, replica_groups=mesh['dp'=16,'mp'=2] {'mp'}, use_global_device_ids=true, to_apply=%region_3.5 | all-reduce | flops 512 | bytes 4096 | tf_op jit(solution)/shard_map/psum | solution.py:90
  92.0 1.3 multiply_convert_fusion.3
  93.3 12.3 %all_gather.15 = bf16[256,1536]{1,0:T(8,128)(2,1)} all-gather(bf16[256,768]{1,0:T(8,128)(2,1)S(1)} %multiply_convert_fusion.3), channel_id=1, replica_groups=mesh['dp'=16,'mp'=2] {'mp'}, dimensions={1}, use_global_device_ids=true | all-gather | bytes 1179648 | tf_op jit(solution)/shard_map/all_gather | solution.py:98
  105.6 2.5 copy.29
  108.1 0.1 all-gather.3.cloned.1.call-done
  108.2 3.3 copy.30
  111.6 1.4 fusion.81
  113.2 0.2 multiply_multiply_fusion.1
  113.4 0.2 copy-done.11
  113.8 3.4 multiply_reduce_fusion
  117.3 24.7 %all-reduce.3 = (f32[768]{0:T(1024)S(1)}, f32[]{:T(128)}, f32[768]{0:T(1024)S(1)}) all-reduce(f32[768]{0:T(1024)S(1)} %get-tuple-element.38, f32[]{:T(128)} %fusion.75, f32[768]{0:T(1024)S(1)} %get-tuple-element.37), channel_id=1, replica_groups=mesh['dp'=16,'mp'=2] {'dp'}, use_global_device_ids=true, to_apply=%region_9.11 | all-reduce | flops 1537 | bytes 12296 | tf_op jit(solution)/shard_map/psum | solution.py:105
  142.0 0.7 broadcast_divide_fusion.1
  142.7 2.2 multiply_convert_fusion.2
  144.8 4.0 fusion.78
  148.9 30.2 %all-reduce.2 = (f32[768]{0:T(1024)S(1)}, f32[768]{0:T(1024)S(1)}) all-reduce(f32[768]{0:T(1024)S(1)} %get-tuple-element.40, f32[768]{0:T(1024)S(1)} %get-tuple-element.39), channel_id=1, replica_groups=mesh['dp'=16,'mp'=2] {'dp'}, use_global_device_ids=true, to_apply=%region_13.15 | all-reduce | flops 1536 | bytes 12288 | tf_op jit(solution)/shard_map/psum | solution.py:134
  179.1 0.7 broadcast_divide_fusion
  179.8 2.4 multiply_reduce_fusion.16
  182.2 2.5 fusion.55
  184.7 0.3 multiply_convert_fusion.1
  185.1 5.0 %fusion.67 = f32[1536,1536]{1,0:T(8,128)} fusion(bf16[256,1536]{1,0:T(8,128)(2,1)S(1)} %copy-done.6, bf16[256,768]{1,0:T(8,128)(2,1)S(1)} %get-tuple-element.89, bf16[256,768]{1,0:T(8,128)(2,1)S(1)} %get-tuple-element.88), kind=kOutput, calls=%fused_computation.136 | convolution fusion | flops 1209532416 | bytes 11010048 | tf_op jit(solution)/shard_map/dot_general | solution.py:45
  190.3 1.0 copy-done.2
  191.3 1.8 multiply_reduce_fusion.1
  193.1 1.0 multiply_reduce_fusion.2
  194.4 2.6 stack.127
  197.0 11.6 %all_gather.17 = bf16[256,1536]{1,0:T(8,128)(2,1)S(1)} all-gather(bf16[256,768]{1,0:T(8,128)(2,1)S(1)} %copy-done.8), channel_id=1, replica_groups=mesh['dp'=16,'mp'=2] {'mp'}, dimensions={1}, use_global_device_ids=true | all-gather | bytes 1179648 | tf_op jit(solution)/shard_map/all_gather | solution.py:121
  208.7 3.1 fusion.82
  211.7 1.2 copy-done.3
  213.0 3.5 fusion.2
  216.4 90.6 %reduce-scatter.3.cloned.1.call-done = f32[96,1536]{1,0:T(8,128)} async-done(((f32[1536,1536]{1,0:T(8,128)}), f32[96,1536]{1,0:T(8,128)}) %reduce-scatter.3.cloned.1.call-update) | async-done | bytes 589840 | tf_op jit(solution)/shard_map/reduce_scatter | solution.py:143
  307.1 2.3 reshape.176
  309.3 88.7 %all-reduce.7.cloned.1.call-done = f32[31,768]{1,0:T(8,128)} async-done(((f32[31,768]{1,0:T(8,128)}), f32[31,768]{1,0:T(8,128)}) %all-reduce.7.cloned.1.call-update) | async-done | bytes 95248 | tf_op jit(solution)/shard_map/psum | solution.py:138
  398.0 78.3 %reduce-scatter.5.cloned.1.call-done = f32[96,768]{1,0:T(8,128)} async-done(((f32[1536,768]{1,0:T(8,128)}), f32[96,768]{1,0:T(8,128)}) %reduce-scatter.5.cloned.1.call-update) | async-done | bytes 294928 | tf_op jit(solution)/shard_map/reduce_scatter | solution.py:125
  476.3 1.5 copy.32
  (115 shorter events, 0.7 us)
Async XLA Ops:
  7.2 56.8 %copy-start = (bf16[320,768]{1,0:T(8,128)(2,1)S(1)}, bf16[320,768]{1,0:T(8,128)(2,1)}, u32[]{:S(2)}) copy-start(bf16[320,768]{1,0:T(8,128)(2,1)} %param.19) | copy-start | bytes 1474564
  7.2 14.6 %copy-start.35 = (s32[1,16]{1,0:T(1,128)S(1)}, s32[1,16]{1,0:T(1,128)}, u32[]{:S(2)}) copy-start(s32[1,16]{1,0:T(1,128)} %param.16) | copy-start | bytes 196
  7.2 52.1 %all-gather.5.cloned.1.call-start = ((), (), s32[]{:S(2)}) async-start(), calls=%async_computation.7 | async-start | bytes 2506752 | tf_op jit(solution)/shard_map/all_gather | solution.py:120
  7.9 14.5 %copy-start.10 = (f32[31,768]{1,0:T(8,128)S(1)}, f32[31,768]{1,0:T(8,128)}, u32[]{:S(2)}) copy-start(f32[31,768]{1,0:T(8,128)} %param.23) | copy-start | bytes 285700
  7.9 15.3 %copy-start.7 = (bf16[256,768]{1,0:T(8,128)(2,1)S(1)}, bf16[256,768]{1,0:T(8,128)(2,1)}, u32[]{:S(2)}) copy-start(bf16[256,768]{1,0:T(8,128)(2,1)} %param.27) | copy-start | bytes 1179652
  7.9 100.2 %all-gather.3.cloned.1.call-start = ((), (), s32[]{:S(2)}) async-start(), calls=%async_computation.6 | async-start | bytes 5013504 | tf_op jit(solution)/shard_map/all_gather | solution.py:96
  12.0 25.3 %all-to-all-start.1 = ((s32[16,1,1]{2,1,0:T(1,128)}), s32[16,1,1]{2,1,0:T(1,128)S(1)}, u32[]{:S(2)}, u32[]{:S(2)}) async-start(s32[16,1,1]{2,1,0:T(1,128)} %copy.27), calls=%async_computation.1 | async-start | bytes 16384 | tf_op jit(solution)/shard_map/all_to_all | solution.py:72
  19.6 34.5 %copy-start.9 = (bf16[128,768]{1,0:T(8,128)(2,1)S(1)}, bf16[128,768]{1,0:T(8,128)(2,1)}, u32[]{:S(2)}) copy-start(bf16[128,768]{1,0:T(8,128)(2,1)} %param.20) | copy-start | bytes 589828
  37.3 10.9 %all-to-all-start.2 = ((s32[16,1,1]{2,1,0:T(1,128)}), s32[16,1,1]{2,1,0:T(1,128)S(1)}, u32[]{:S(2)}, u32[]{:S(2)}) async-start(s32[16,1,1]{2,1,0:T(1,128)} %copy.28), calls=%async_computation.2 | async-start | bytes 16384 | tf_op jit(solution)/shard_map/all_to_all | solution.py:73
  43.9 9.6 %copy-start.28 = (f32[256]{0:T(256)}, f32[256]{0:T(256)S(1)}, u32[]{:S(2)}) copy-start(f32[256]{0:T(256)S(1)} %reshape.177) | copy-start | bytes 3076
  48.2 11.0 %all-to-all-start = ((bf16[16,16,320]{2,1,0:T(8,128)(2,1)}), bf16[16,16,320]{2,1,0:T(8,128)(2,1)S(1)}, u32[]{:S(2)}, u32[]{:S(2)}) async-start(bf16[16,16,320]{2,1,0:T(8,128)(2,1)} %broadcast_select_fusion), calls=%async_computation | async-start | bytes 393216 | tf_op jit(solution)/shard_map/all_to_all | solution.py:71
  59.3 46.3 %all-to-all-start.3 = ((bf16[2,768,768]{2,1,0:T(8,128)(2,1)}), bf16[2,768,768]{2,1,0:T(8,128)(2,1)S(1)}, u32[]{:S(2)}, u32[]{:S(2)}) async-start(bf16[2,768,768]{2,1,0:T(8,128)(2,1)} %bitcast.84), calls=%async_computation.3 | async-start | bytes 4718592 | tf_op jit(solution)/shard_map/all_to_all | solution.py:129
  63.1 244.0 %reduce-scatter.3.cloned.1.call-start = ((), (), s32[]{:S(2)}) async-start(), calls=%async_computation.8 | async-start | bytes 10027008 | tf_op jit(solution)/shard_map/reduce_scatter | solution.py:143
  63.9 28.0 %copy-start.31 = (f32[768]{0:T(1024)S(1)}, f32[768]{0:T(1024)}, u32[]{:S(2)}) copy-start(f32[768]{0:T(1024)} %param.21) | copy-start | bytes 9220
  108.2 3.4 copy-start.5
  111.6 1.4 copy-start.29
  113.0 0.7 copy-start.11
  113.0 0.7 copy-start.12
  113.0 0.7 copy-start.13
  113.0 0.7 copy-start.14
  113.0 0.7 copy-start.15
  113.0 0.7 copy-start.16
  113.0 0.7 copy-start.17
  113.0 0.7 copy-start.18
  113.0 0.7 copy-start.19
  113.1 0.7 copy-start.20
  113.1 0.7 copy-start.21
  113.1 0.7 copy-start.22
  113.1 0.7 copy-start.23
  113.1 0.7 copy-start.24
  113.1 0.7 copy-start.25
  113.1 0.7 copy-start.26
  113.1 0.7 copy-start.27
  113.1 29.5 %copy-start.30 = (f32[768]{0:T(1024)S(1)}, f32[768]{0:T(1024)}, u32[]{:S(2)}) copy-start(f32[768]{0:T(1024)} %param.24) | copy-start | bytes 9220
  113.1 29.5 %copy-start.32 = (f32[768]{0:T(1024)S(1)}, f32[768]{0:T(1024)}, u32[]{:S(2)}) copy-start(f32[768]{0:T(1024)} %param.25) | copy-start | bytes 9220
  144.8 4.0 copy-start.4
  179.1 5.6 %copy-start.33 = (f32[768]{0:T(1024)}, f32[768]{0:T(1024)S(1)}, u32[]{:S(2)}) copy-start(f32[768]{0:T(1024)S(1)} %get-tuple-element.101) | copy-start | bytes 9220
  179.1 5.6 %copy-start.34 = (f32[768]{0:T(1024)}, f32[768]{0:T(1024)S(1)}, u32[]{:S(2)}) copy-start(f32[768]{0:T(1024)S(1)} %get-tuple-element.100) | copy-start | bytes 9220
  182.2 2.9 copy-start.1
  182.2 2.9 copy-start.6
  190.2 1.1 copy-start.2
  190.2 6.8 %copy-start.8 = (bf16[256,768]{1,0:T(8,128)(2,1)S(1)}, bf16[256,768]{1,0:T(8,128)(2,1)}, u32[]{:S(2)}) copy-start(bf16[256,768]{1,0:T(8,128)(2,1)} %get-tuple-element.83) | copy-start | bytes 1179652
  190.2 207.8 %all-reduce.7.cloned.1.call-start = ((), (), s32[]{:S(2)}) async-start(), calls=%async_computation.10 | async-start | bytes 196608 | tf_op jit(solution)/shard_map/psum | solution.py:138
  208.6 267.7 %reduce-scatter.5.cloned.1.call-start = ((), (), s32[]{:S(2)}) async-start(), calls=%async_computation.9 | async-start | bytes 5013504 | tf_op jit(solution)/shard_map/reduce_scatter | solution.py:125
  211.7 1.2 copy-start.3
Sparse Core Ops, SparseCore 0:
  10.3 42.9 all-gather.4
  55.6 52.5 all-gather.2
  190.3 116.7 reduce-scatter.2
  311.3 86.6 all-reduce.6
  402.3 74.0 reduce-scatter.4
where the time goes:
time: 487 us; the launch traced here: 484 us
  waiting for transfers between devices  268 us (55%)
  blocking collectives  117 us (24%)
  local copies, waits for them, and re-layouts  23.5 us (5%)
  other arithmetic  21.4 us (4%)
  starting transfers between devices  21.2 us (4%)
  matrix products  18.4 us (4%)
  between operations  14.5 us (3%)
    reduce_scatter x1, waiting for transfers between devices, on_device(): lax.psum_scatter(contract_rows(normed_full, dpre), 'dp', scatter_dimensio...  90.6 us
    psum x1, waiting for transfers between devices, on_device(): lax.psum(kernel_terms(dconv, glu_out, kernel.shape[0], frames), 'dp')  88.7 us
    reduce_scatter x1, waiting for transfers between devices, on_device(): lax.psum_scatter(contract_rows(hidden_full, cotangent), 'dp', scatter_dim...  78.3 us
    psum x1, blocking collectives, on_device(): lax.psum((jnp.sum(dact, 0), jnp.sum(dact * normed_conv, 0)), 'dp')  30.2 us
    psum x1, blocking collectives, on_device(): lax.psum((jnp.sum(inputs, 1), jnp.sum(inputs * inputs, 1)), 'mp')  26.7 us
    psum x1, blocking collectives, on_device(): lax.psum((jnp.sum(valid_col * conv_out, 0), jnp.sum(valid_col * conv_out...  24.7 us
    all_gather x1, blocking collectives, on_device(): normed_full = lax.all_gather(normed_in, 'mp', axis=1, tiled=True)  12.3 us
    all_gather x1, blocking collectives, on_device(): cot_full = lax.all_gather(cotangent, 'mp', axis=1, tiled=True)  11.9 us
  transfers between devices with their start and end apart: 9, of which 6 were waited for; matrix products, arithmetic and copies ran while one was open for 7% of the time, Pallas kernels for 0%

commit v1 on v0

v1 whole, which is shorter than its diff:
```python
import functools

import jax
import jax.numpy as jnp
from jax import lax
from jax.experimental import pallas as pl
from jax.experimental.pallas import tpu as pltpu
from jax.sharding import PartitionSpec as P

EPS = 1e-05


def depth_conv(values, taps, frames):
    chans = values.shape[1]
    shaped = values.reshape(-1, frames, chans)
    margin = taps.shape[0] // 2
    padded = jnp.pad(shaped, ((0, 0), (margin, margin), (0, 0)))
    total = jnp.zeros(shaped.shape, jnp.float32)
    for step in range(taps.shape[0]):
        total = total + taps[step] * padded[:, step : step + frames]
    return total.reshape(values.shape)


def depth_back(grads, taps, frames):
    chans = grads.shape[1]
    shaped = grads.reshape(-1, frames, chans)
    margin = taps.shape[0] // 2
    padded = jnp.pad(shaped, ((0, 0), (margin, margin), (0, 0)))
    total = jnp.zeros(shaped.shape, jnp.float32)
    for step in range(taps.shape[0]):
        begin = 2 * margin - step
        total = total + taps[step] * padded[:, begin : begin + frames]
    return total.reshape(grads.shape)


def kernel_terms(grads, values, width, frames):
    chans = values.shape[1]
    shaped = values.reshape(-1, frames, chans)
    grad_shaped = grads.reshape(-1, frames, chans)
    margin = width // 2
    padded = jnp.pad(shaped, ((0, 0), (margin, margin), (0, 0)))
    rows_out = []
    for step in range(width):
        rows_out.append(jnp.sum(grad_shaped * padded[:, step : step + frames], axis=(0, 1)))
    return jnp.stack(rows_out, 0)


def contract_rows(left, right):
    return lax.dot_general(
        left, right, (((0,), (0,)), ((), ())), preferred_element_type=jnp.float32
    )


MESH = pl.DeviceIdType.MESH
F32 = jnp.float32
BF16 = jnp.bfloat16
VMEM = pl.BlockSpec(memory_space=pltpu.VMEM)
DMA = pltpu.SemaphoreType.DMA
LIMIT = 56 * 1024 * 1024


def greet(axes):
    barrier = pltpu.get_barrier_semaphore()
    total = 0
    for axis in axes:
        size, me = lax.axis_size(axis), lax.axis_index(axis)
        for k in range(1, size):
            pl.semaphore_signal(
                barrier, inc=1, device_id={axis: lax.rem(me + k, size)}, device_id_type=MESH
            )
        total += size - 1
    pl.semaphore_wait(barrier, total)


def push(src, dst, send, recv, axis, peer):
    copy = pltpu.make_async_remote_copy(
        src_ref=src,
        dst_ref=dst,
        send_sem=send,
        recv_sem=recv,
        device_id={axis: peer},
        device_id_type=MESH,
    )
    copy.start()
    return copy


def push_all(axis, source, slots, send, recv):
    size, me = lax.axis_size(axis), lax.axis_index(axis)
    copies = []
    for k in range(1, size):
        peer = lax.rem(me + k, size)
        copies.append(push(source(peer), slots.at[me], send.at[k], recv.at[k], axis, peer))
    return copies


def sum_slots(slots, size):
    total = slots[0]
    for p in range(1, size):
        total = total + slots[p]
    return total


def stats_kernel(x_ref, o_ref, slots, send, recv):
    size, me = lax.axis_size("dp"), lax.axis_index("dp")
    greet(("dp",))
    copies = push_all("dp", lambda peer: x_ref, slots, send, recv)
    slots[me] = x_ref[...]
    for copy in copies:
        copy.wait()
    o_ref[...] = sum_slots(slots, size)


def stats_sum(row, cid):
    n = lax.axis_size("dp")
    return pl.pallas_call(
        stats_kernel,
        out_shape=jax.ShapeDtypeStruct(row.shape, F32),
        in_specs=[VMEM],
        out_specs=VMEM,
        scratch_shapes=[pltpu.VMEM((n,) + row.shape, F32), DMA((n,)), DMA((n,))],
        compiler_params=pltpu.CompilerParams(collective_id=cid, has_side_effects=True),
        name="stats_sum",
    )(row)


def stats_hidden_kernel(
    x_ref, h_ref, o_ref, hid_ref, slots, hslots, send, recv, hsend, hrecv
):
    size, me = lax.axis_size("dp"), lax.axis_index("dp")
    parts, mine = lax.axis_size("mp"), lax.axis_index("mp")
    chans = h_ref.shape[1]
    greet(("dp", "mp"))
    copies = push_all("dp", lambda peer: x_ref, slots, send, recv)
    wide = push_all("mp", lambda peer: h_ref, hslots, hsend, hrecv)
    slots[me] = x_ref[...]
    hslots[mine] = h_ref[...]
    for copy in copies:
        copy.wait()
    o_ref[...] = sum_slots(slots, size)
    for copy in wide:
        copy.wait()
    for p in range(parts):
        hid_ref[:, p * chans : (p + 1) * chans] = hslots[p]


def stats_hidden(row, hidden, cid):
    n, q = lax.axis_size("dp"), lax.axis_size("mp")
    rows, chans = hidden.shape
    return pl.pallas_call(
        stats_hidden_kernel,
        out_shape=(
            jax.ShapeDtypeStruct(row.shape, F32),
            jax.ShapeDtypeStruct((rows, q * chans), BF16),
        ),
        in_specs=[VMEM, VMEM],
        out_specs=(VMEM, VMEM),
        scratch_shapes=[
            pltpu.VMEM((n,) + row.shape, F32),
            pltpu.VMEM((q,) + hidden.shape, BF16),
            DMA((n,)),
            DMA((n,)),
            DMA((q,)),
            DMA((q,)),
        ],
        compiler_params=pltpu.CompilerParams(
            collective_id=cid, has_side_effects=True, vmem_limit_bytes=LIMIT
        ),
        name="stats_hidden",
    )(row, hidden)


def grads_kernel(
    n,
    g1,
    g2,
    gk,
    o1,
    o2,
    ok,
    r1a,
    r1b,
    s1a,
    acc1,
    r2a,
    s2a,
    r3a,
    s1b,
    r2b,
    acc2,
    s2b,
    r3b,
    kslots,
    ksum,
    kall,
    core_sem,
    xa_sem,
    za_sem,
    zb_sem,
    xb_sem,
    k_sem,
    k2_sem,
):
    m = n // 4
    me = lax.axis_index("dp")
    c = lax.rem(me, 2)
    b = lax.rem(me // 2, 2)
    a = me // 4
    core_peer = me + 1 - 2 * c
    x_peer = me + 2 - 4 * b
    greet(("dp",))

    copy_1a = push(g1.at[:, :, 1 - c], r1a, core_sem.at[0, 0], core_sem.at[1, 0], "dp", core_peer)
    copy_1b = push(g2.at[:, :, 1 - c], r1b, core_sem.at[0, 1], core_sem.at[1, 1], "dp", core_peer)
    k_copies = push_all("dp", lambda peer: gk.at[peer], kslots, k_sem.at[0], k_sem.at[1])
    kslots[me] = gk[me]

    order = [lax.rem(a + k, m) for k in range(m)]
    steps = list(range(1, m)) + [0]

    copy_1a.wait_recv()
    xa = {}
    for k in steps:
        to = order[k]
        s1a[to] = (
            g1[to, 1 - b, c].astype(F32) + r1a[to, 1 - b].astype(F32)
        ).astype(BF16)
        xa[k] = push(s1a.at[to], r2a.at[to], xa_sem.at[0, k], xa_sem.at[1, k], "dp", x_peer)
    copy_1b.wait_recv()
    zb = []
    for k in steps:
        to = order[k]
        if k == 0:
            for j in range(2):
                acc2[j] = g2[to, j, c].astype(F32) + r1b[to, j].astype(F32)
            continue
        for j in range(2):
            s1b[to, j] = (g2[to, j, c].astype(F32) + r1b[to, j].astype(F32)).astype(BF16)
        peer = to * 4 + b * 2 + c
        zb.append(push(s1b.at[to], r2b.at[a], zb_sem.at[0, k], zb_sem.at[1, k], "dp", peer))
    for k in steps:
        to = order[k]
        acc1[to] = g1[to, b, c].astype(F32) + r1a[to, b].astype(F32)

    for copy in k_copies:
        copy.wait()
    ksum[...] = sum_slots(kslots, n)
    k2_copies = push_all("dp", lambda peer: ksum, kall, k2_sem.at[0], k2_sem.at[1])
    kall[me] = ksum[...]

    za = []
    for k in steps:
        to = order[k]
        xa[k].wait()
        if k == 0:
            continue
        s2a[to] = (acc1[to] + r2a[to].astype(F32)).astype(BF16)
        peer = to * 4 + b * 2 + c
        za.append(push(s2a.at[to], r3a.at[a], za_sem.at[0, k], za_sem.at[1, k], "dp", peer))

    for copy in zb:
        copy.wait()
    for k in range(1, m):
        frm = lax.rem(a - k + m, m)
        for j in range(2):
            acc2[j] = acc2[j] + r2b[frm, j].astype(F32)
    s2b[...] = acc2[1 - b].astype(BF16)
    xb = push(s2b, r3b, xb_sem.at[0], xb_sem.at[1], "dp", x_peer)

    o1[...] = acc1[a] + r2a[a].astype(F32)
    for copy in k2_copies:
        copy.wait()
    ok[...] = kall[...]
    xb.wait()
    o2[...] = acc2[b] + r3b[...].astype(F32)
    for copy in za:
        copy.wait()
    total = o1[...]
    for k in range(1, m):
        total = total + r3a[lax.rem(a - k + m, m)].astype(F32)
    o1[...] = total
    copy_1a.wait_send()
    copy_1b.wait_send()


def grads_sum(g1, g2, gk, cid):
    n = lax.axis_size("dp")
    m = n // 4
    rows, wide = g1.shape[0] // n, g1.shape[1]
    chans = g2.shape[1]
    flat = gk.reshape(-1)
    part = -(-flat.shape[0] // (n * 128)) * 128
    flat = jnp.pad(flat, (0, n * part - flat.shape[0])).reshape(n, 1, part)
    o1, o2, ok = pl.pallas_call(
        functools.partial(grads_kernel, n),
        out_shape=(
            jax.ShapeDtypeStruct((rows, wide), F32),
            jax.ShapeDtypeStruct((rows, chans), F32),
            jax.ShapeDtypeStruct((n, 1, part), F32),
        ),
        in_specs=[VMEM] * 3,
        out_specs=(VMEM,) * 3,
        scratch_shapes=[
            pltpu.VMEM((m, 2, rows, wide), BF16),
            pltpu.VMEM((m, 2, rows, chans), BF16),
            pltpu.VMEM((m, rows, wide), BF16),
            pltpu.VMEM((m, rows, wide), F32),
            pltpu.VMEM((m, rows, wide), BF16),
            pltpu.VMEM((m, rows, wide), BF16),
            pltpu.VMEM((m, rows, wide), BF16),
            pltpu.VMEM((m, 2, rows, chans), BF16),
            pltpu.VMEM((m, 2, rows, chans), BF16),
            pltpu.VMEM((2, rows, chans), F32),
            pltpu.VMEM((rows, chans), BF16),
            pltpu.VMEM((rows, chans), BF16),
            pltpu.VMEM((n, 1, part), F32),
            pltpu.VMEM((1, part), F32),
            pltpu.VMEM((n, 1, part), F32),
            DMA((2, 2)),
            DMA((2, m)),
            DMA((2, m)),
            DMA((2, m)),
            DMA((2,)),
            DMA((2, n)),
            DMA((2, n)),
        ],
        compiler_params=pltpu.CompilerParams(
            collective_id=cid, has_side_effects=True, vmem_limit_bytes=LIMIT
        ),
        name="grads_sum",
    )(
        g1.reshape(m, 2, 2, rows, wide),
        g2.reshape(m, 2, 2, rows, chans),
        flat,
    )
    return o1, o2, ok.reshape(-1)[: gk.size].reshape(gk.shape)


def on_device(
    corpus,
    picks,
    lengths,
    langs,
    w_in,
    lang_table,
    ln_gain,
    w_pw1,
    kernel,
    bn_gain,
    bn_bias,
    w_pw2,
    cotangent,
):
    model_width = w_pw2.shape[0] * lax.axis_size("dp")
    parts = lax.axis_size("mp")
    weights_one = lax.all_gather(w_pw1, "dp", axis=0, tiled=True).reshape(model_width, -1)
    half = weights_one.shape[1] // 2
    feats = corpus.shape[2]
    frames = corpus.shape[1]
    picked = picks[0][:, None] == jnp.arange(corpus.shape[0], dtype=jnp.int32)[None, :]
    blocks = jnp.einsum(
        "sb,bfk->sfk", picked.astype(BF16), corpus, preferred_element_type=F32
    ).astype(BF16)
    lens_send = jnp.sum(jnp.where(picked, lengths[None, :], 0), 1)
    lang_send = jnp.sum(jnp.where(picked, langs[None, :], 0), 1)
    whole = jnp.stack([lens_send, lang_send], 1).astype(BF16)
    whole = jnp.broadcast_to(whole[:, None, :], (whole.shape[0], frames, 2))
    packed = jnp.concatenate([blocks, whole], 2)
    received = lax.all_to_all(packed, "dp", split_axis=0, concat_axis=0, tiled=True)
    lens = received[:, 0, feats].astype(jnp.int32)
    lang = received[:, 0, feats + 1].astype(jnp.int32)
    valid = (
        (jnp.arange(frames, dtype=jnp.int32)[None, :] < lens[:, None]).astype(F32).reshape(-1)
    )
    valid_col = valid[:, None]
    mel = received[:, :, :feats].reshape(-1, feats) * valid_col.astype(BF16)
    onehot = (lang[:, None] == jnp.arange(lang_table.shape[0], dtype=jnp.int32)[None, :]).astype(
        BF16
    )
    onehot = jnp.repeat(onehot, frames, axis=0)
    left = jnp.concatenate([mel, onehot], 1)
    right = jnp.concatenate([w_in, lang_table], 0)
    right_full = lax.all_gather(right, "mp", axis=1, tiled=True)
    gain_full = lax.all_gather(ln_gain, "mp", axis=0, tiled=True)
    inputs = jnp.dot(left, right, preferred_element_type=F32)
    full_in = jnp.dot(left, right_full, preferred_element_type=F32)
    mean = jnp.sum(full_in, 1) / model_width
    var = jnp.sum(full_in * full_in, 1) / model_width - mean * mean
    normed_full = (
        (full_in - mean[:, None]) * lax.rsqrt(var + EPS)[:, None] * gain_full
    ).astype(BF16)
    pre = jnp.dot(normed_full, weights_one, preferred_element_type=jnp.float32)
    linear_part = pre[:, :half]
    gate_part = pre[:, half:]
    gate_sig = jax.nn.sigmoid(gate_part)
    glu_out = linear_part * gate_sig * valid_col
    conv_out = depth_conv(glu_out, kernel, frames)
    row = jnp.concatenate(
        [
            jnp.sum(valid_col * conv_out, 0),
            jnp.sum(valid_col * conv_out * conv_out, 0),
            jnp.full((128,), jnp.sum(valid), F32),
        ]
    )[None]
    row = stats_sum(row, 1)
    sum_conv, sum_sq, count = row[0, :half], row[0, half : 2 * half], row[0, 2 * half]
    mu_conv = sum_conv / count
    var_conv = sum_sq / count - mu_conv * mu_conv
    inv_std = lax.rsqrt(var_conv + EPS)
    normed_conv = (conv_out - mu_conv) * inv_std
    act = normed_conv * bn_gain + bn_bias
    act_sig = jax.nn.sigmoid(act)
    hidden = (valid_col * act * act_sig).astype(jnp.bfloat16)
    w_later, _ = lax.optimization_barrier((w_pw2, weights_one))
    weights_two = lax.all_gather(w_later, "dp", axis=0, tiled=True)
    partial = lax.dot_general(
        cotangent, weights_two, (((1,), (1,)), ((), ())), preferred_element_type=F32
    ).astype(BF16)
    partial = jnp.stack([partial[:, p * half : (p + 1) * half] for p in range(parts)], 0)
    partial = lax.all_to_all(partial, "mp", split_axis=0, concat_axis=0, tiled=True)
    dhidden = jnp.sum(partial.astype(F32), 0)
    dact = dhidden * valid_col * act_sig * (1.0 + act * (1.0 - act_sig))
    row2 = jnp.concatenate([jnp.sum(dact, 0), jnp.sum(dact * normed_conv, 0)])[None]
    row2, hidden_full = stats_hidden(row2, hidden, 2)
    grad_bias, grad_gain = row2[0, :half], row2[0, half:]
    encoded = (inputs + jnp.dot(hidden_full, weights_two, preferred_element_type=F32)).astype(
        BF16
    )
    part_pw2 = contract_rows(hidden_full, cotangent).astype(BF16)
    dconv = (
        valid_col * inv_std * bn_gain * (dact - grad_bias / count - normed_conv * grad_gain / count)
    )
    part_kernel = kernel_terms(dconv, glu_out, kernel.shape[0], frames)
    dglu = depth_back(dconv, kernel, frames)
    dlin = dglu * valid_col * gate_sig
    dgate = dglu * valid_col * linear_part * gate_sig * (1.0 - gate_sig)
    dpre = jnp.concatenate([dlin, dgate], 1).astype(jnp.bfloat16)
    part_pw1 = contract_rows(normed_full, dpre).astype(BF16)
    grad_pw1, grad_pw2, grad_kernel = grads_sum(part_pw1, part_pw2, part_kernel, 3)
    grad_pw1 = grad_pw1.reshape(grad_pw1.shape[0], 2, half)
    return (encoded, grad_pw1, grad_pw2, grad_kernel, grad_gain, grad_bias)


def solution(mesh):
    return jax.shard_map(
        on_device,
        mesh=mesh,
        in_specs=(
            P("dp", None, None),
            P("dp", None),
            P("dp"),
            P("dp"),
            P(None, "mp"),
            P(None, "mp"),
            P("mp"),
            P("dp", None, "mp"),
            P(None, "mp"),
            P("mp"),
            P("mp"),
            P("dp", "mp"),
            P("dp", "mp"),
        ),
        out_specs=(
            P("dp", "mp"),
            P("dp", None, "mp"),
            P("dp", "mp"),
            P(None, "mp"),
            P("mp"),
            P("mp"),
        ),
        check_vma=False,
    )
```

time: 487 us -> 284 us (0.58)
  waiting for transfers between devices: 268 us -> 92.6 us
  blocking collectives: 117 us -> 4.38 us
  Pallas kernels: 0 us -> 93 us
  starting transfers between devices: 21.2 us -> 8.28 us
  other arithmetic: 21.4 us -> 27.7 us
    reduce_scatter x2 -> x0, waiting for transfers between devices: 169 us -> none  [the longest x1 90.6 us: on_device(): lax.psum_scatter(contract_rows(normed_full, dpre), 'dp', scatter_dimensio...]
    pallas_call x0 -> x3, Pallas kernels: none -> 93 us  [the longest x1 68.6 us: grads_sum(): pl.pallas_call(functools.partial(grads_kernel, n), out_shape=(jax.ShapeDt...]
    psum x1 -> x0, waiting for transfers between devices: 88.7 us -> none  [on_device(): lax.psum(kernel_terms(dconv, glu_out, kernel.shape[0], frames), 'dp')]
    psum x3 -> x0, blocking collectives: 81.6 us -> none  [the longest x1 30.2 us: on_device(): lax.psum((jnp.sum(dact, 0), jnp.sum(dact * normed_conv, 0)), 'dp')]
    all_gather x1, waiting for transfers between devices: 0.14 us -> 53.8 us  [on_device(): lax.all_gather(w_pw1, 'dp', axis=0, tiled=True).reshape(model_width, -1)]
    all_gather x1 -> x2, waiting for transfers between devices: 0.01 us -> 37.7 us  [the longest x1 31.6 us: on_device(): weights_two = lax.all_gather(w_later, 'dp', axis=0, tiled=True)]
    all_gather x3 -> x1, blocking collectives: 35.8 us -> 4.38 us  [on_device(): gain_full = lax.all_gather(ln_gain, 'mp', axis=0, tiled=True)]
    all_to_all x4 -> x2, starting transfers between devices: 21 us -> 8.16 us  [the longest x1 4.31 us: on_device(): lax.all_to_all(partial, 'mp', split_axis=0, concat_axis=0, tiled=True)]
  transfers between devices with their start and end apart: 9 -> 5, of which waited for: 6 -> 4; matrix products, arithmetic and copies ran while one was open for 7% -> 10% of each run, Pallas kernels for 0% -> 3%
where the time goes in v1:
time: 284 us; the launch traced here: 283 us
  Pallas kernels  93 us (33%)
  waiting for transfers between devices  92.6 us (33%)
  other arithmetic  27.7 us (10%)
  local copies, waits for them, and re-layouts  24.4 us (9%)
  matrix products  16.9 us (6%)
  between operations  15.3 us (5%)
  starting transfers between devices  8.28 us (3%)
  blocking collectives  4.38 us (2%)
    pallas_call x1, Pallas kernels, grads_sum(): pl.pallas_call(functools.partial(grads_kernel, n), out_shape=(jax.ShapeDt...  68.6 us
    all_gather x1, waiting for transfers between devices, on_device(): lax.all_gather(w_pw1, 'dp', axis=0, tiled=True).reshape(model_width, -1)  53.8 us
    all_gather x1, waiting for transfers between devices, on_device(): weights_two = lax.all_gather(w_later, 'dp', axis=0, tiled=True)  31.6 us
    pallas_call x1, Pallas kernels, stats_hidden(): pl.pallas_call(stats_hidden_kernel, out_shape=(jax.ShapeDtypeStruct(row.s...  16.2 us
    unnamed x189, local copies, waits for them, and re-layouts  11.9 us
    pallas_call x1, Pallas kernels, stats_sum(): pl.pallas_call(stats_kernel, out_shape=jax.ShapeDtypeStruct(row.shape, F3...  8.14 us
    all_gather x1, waiting for transfers between devices, on_device(): right_full = lax.all_gather(right, 'mp', axis=1, tiled=True)  6.11 us
    dot_general x2, matrix products, contract_rows(): lax.dot_general(left, right, (((0,), (0,)), ((), ())), preferred_element_...  6 us
  transfers between devices with their start and end apart: 5, of which 4 were waited for; matrix products, arithmetic and copies ran while one was open for 10% of the time, Pallas kernels for 3%

profile of v1, /device:TPU:8, one launch (start us, length us, event | category | flops | bytes accessed | tf_op | source)
XLA Modules:
  0.0 282.6 jit_solution(388827484688021908)
XLA Ops:
  7.2 0.7 all-gather.5.cloned.1.call-update
  8.0 1.1 constant_dynamic-update-slice_fusion.1
  9.0 0.9 constant_dynamic-update-slice_fusion
  10.0 0.9 copy-done.4
  10.9 53.8 %all-gather.5.cloned.1.call-done = bf16[1536,2,768]{2,1,0:T(2,128)(2,1)} async-done(((bf16[96,2,768]{2,1,0:T(2,128)(2,1)}), bf16[1536,2,768]{2,1,0:T(2,128)(2,1)}) %all-gather.5.cloned.1.call-update) | async-done | bytes 4718608 | tf_op jit(solution)/shard_map/all_gather | solution.py:356
  64.8 5.4 %copy.28 = bf16[192,8,2,768]{3,1,2,0:T(8,128)(2,1)} copy(bf16[192,8,2,768]{3,2,1,0:T(2,128)(2,1)} %bitcast.61) | data formatting | bytes 9437184
  70.2 0.2 select_reduce_fusion.1
  70.5 0.1 copy.25
  70.6 0.6 convolution_convert_fusion.3
  71.2 0.1 pad_maximum_fusion.2
  71.3 0.7 copy.26
  72.0 3.8 %all-to-all-start = ((bf16[16,16,322]{2,1,0:T(8,128)(2,1)}), bf16[16,16,322]{2,1,0:T(8,128)(2,1)S(1)}, u32[]{:S(2)}, u32[]{:S(2)}) async-start(bf16[16,16,322]{2,1,0:T(8,128)(2,1)} %copy.26), calls=%async_computation | async-start | bytes 393216 | tf_op jit(solution)/shard_map/all_to_all | solution.py:369
  75.9 4.4 %all-gather = f32[2,1,768]{2,1,0:T(1,128)S(1)} all-gather(f32[1,1,768]{2,1,0:T(1,128)S(1)} %reshape.287), channel_id=1, replica_groups=mesh['dp'=16,'mp'=2] {'mp'}, dimensions={0}, use_global_device_ids=true | all-gather | bytes 9216 | tf_op jit(solution)/shard_map/all_gather | solution.py:384
  80.3 0.7 slice_reduce_fusion.30
  81.0 0.8 slice_reduce_fusion.31
  81.8 0.3 all-to-all-done
  82.0 0.7 fusion.74
  82.8 0.1 fusion.77
  82.8 0.1 reshape.285
  82.9 0.7 fusion.80
  83.6 0.1 fusion.78
  83.7 0.1 bitcast_multiply_fusion.1
  83.8 6.1 %all-gather.9.cloned.1.call-done = bf16[448,1536]{1,0:T(8,128)(2,1)} async-done(((bf16[448,768]{1,0:T(8,128)(2,1)}), bf16[448,1536]{1,0:T(8,128)(2,1)}) %all-gather.9.cloned.1.call-update) | async-done | bytes 1376272 | tf_op jit(solution)/shard_map/all_gather | solution.py:383
  89.9 2.0 fusion.85
  92.0 0.6 copy-done.83
  92.6 3.8 %fusion.84 = f32[256,1536]{1,0:T(8,128)S(1)} fusion(bf16[1536,1536]{1,0:T(8,128)(2,1)} %bitcast.60, f32[256,1536]{1,0:T(8,128)S(1)} %get-tuple-element.104, f32[1536]{0:T(1024)S(1)} %reshape.288, f32[256]{0:T(256)S(1)} %get-tuple-element.103, f32[256]{0:T(256)S(1)} %get-tuple-element.102), kind=kOutput, calls=%fused_computation.255 | convolution fusion | flops 1209532416 | bytes 7872512 | tf_op jit(solution)/shard_map/dot_general | solution.py:392
  96.8 0.2 multiply_multiply_fusion.1
  97.0 1.0 copy-done.1
  98.3 4.1 %multiply_reduce_fusion.1 = (f32[768]{0:T(1024)}, f32[768]{0:T(1024)}, f32[16,16,768]{2,1,0:T(8,128)}) fusion(f32[16,16]{1,0:T(8,128)S(1)} %fusion.77, f32[768]{0:T(1024)S(1)} %copy-done.74, f32[768]{0:T(1024)S(1)} %copy-done.76, f32[768]{0:T(1024)S(1)} %copy-done.18, f32[768]{0:T(1024)S(1)} %copy-done.20, f32[768]{0:T(1024)S(1)} %copy-done.22, ...), kind=kLoop, calls=%fused_computation.71 | loop fusion | flops 12777984 | bytes 1675264 | tf_op jit(solution)/shard_map/reduce_sum | solution.py:400
  102.4 31.6 %all-gather.7.cloned.1.call-done = bf16[1536,768]{1,0:T(8,128)(2,1)} async-done(((bf16[96,768]{1,0:T(8,128)(2,1)}), bf16[1536,768]{1,0:T(8,128)(2,1)}) %all-gather.7.cloned.1.call-update) | async-done | bytes 2359312 | tf_op jit(solution)/shard_map/all_gather | solution.py:415
  134.0 2.5 fusion
  136.5 0.1 slice_bitcast_fusion.1
  136.6 0.9 pad_maximum_fusion
  137.5 4.3 %all-to-all-start.1 = ((bf16[2,256,768]{1,2,0:T(8,128)(2,1)}), bf16[2,256,768]{1,2,0:T(8,128)(2,1)}, u32[]{:S(2)}, u32[]{:S(2)}) async-start(bf16[2,256,768]{1,2,0:T(8,128)(2,1)} %pad_maximum_fusion), calls=%async_computation.1 | async-start | bytes 1572864 | tf_op jit(solution)/shard_map/all_to_all | solution.py:420
  141.8 0.6 broadcast_in_dim.58
  142.5 0.7 pad_maximum_fusion.5
  143.2 0.6 broadcast_in_dim.59.x_ref
  143.8 8.1 %stats_sum.1 = f32[1,1664]{1,0:T(1,128)} custom-call(f32[1,1664]{1,0:T(1,128)} %broadcast_in_dim.59.x_ref), custom_call_target="tpu_custom_call" | custom-call | tf_op jit(solution)/shard_map/stats_sum/pallas_call | solution.py:116
  151.9 1.1 slice.448
  153.1 1.3 fusion.87
  154.3 0.6 copy-done.11
  154.9 2.2 multiply_convert_fusion.3.h_ref
  157.1 2.2 convert_reduce_fusion
  159.3 2.3 copy.27
  161.6 2.0 fusion.86
  163.6 0.6 broadcast_in_dim.60.x_ref
  164.2 16.2 %stats_hidden.1 = (f32[1,1536]{1,0:T(1,128)}, bf16[256,1536]{1,0:T(8,128)(2,1)}) custom-call(f32[1,1536]{1,0:T(1,128)} %broadcast_in_dim.60.x_ref, bf16[256,768]{1,0:T(8,128)(2,1)} %multiply_convert_fusion.3.h_ref), custom_call_target="tpu_custom_call" | custom-call | tf_op jit(solution)/shard_map/stats_hidden/pallas_call | solution.py:150
  180.5 1.9 slice_reduce_fusion.32
  182.4 2.8 multiply_reduce_fusion.2
  185.5 1.5 multiply_reduce_fusion.21
  187.3 3.3 %fusion.54 = f32[16,16,768]{2,1,0:T(8,128)} fusion(f32[16,16,768]{2,1,0:T(8,128)S(1)} %get-tuple-element.95, f32[768]{0:T(1024)S(1)} %copy-done.75, f32[768]{0:T(1024)S(1)} %copy-done.77, f32[768]{0:T(1024)S(1)} %copy-done.19, f32[768]{0:T(1024)S(1)} %copy-done.21, f32[768]{0:T(1024)S(1)} %copy-done.23, f32[768]{0:T(1024)S(1)} %copy-done.25, ...), kind=kLoop, calls=%fused_computation.124 | loop fusion | flops 11993088 | bytes 1668096 | tf_op jit(solution)/shard_map/add | solution.py:32
  190.6 2.3 convolution_convert_fusion.1
  192.9 0.8 fusion.88
  193.7 0.3 copy-done.5
  194.0 1.1 fusion.1
  195.5 0.2 stack.151
  195.7 1.6 multiply_convert_fusion.2
  197.3 0.6 pad.14
  198.0 3.7 %convolution_convert_fusion = bf16[1536,1536]{1,0:T(8,128)(2,1)} fusion(bf16[256,768]{1,0:T(8,128)(2,1)S(1)} %get-tuple-element.99, bf16[256,768]{1,0:T(8,128)(2,1)S(1)} %get-tuple-element.98, f32[256,1536]{1,0:T(8,128)S(1)} %copy-done.7, f32[1536]{0:T(1024)S(1)} %reshape.288, f32[256]{0:T(256)S(1)} %copy-done.86, f32[256]{0:T(256)S(1)} %copy-done.84), kind=kOutput, calls=%fused_computation.60 | convolution fusion | flops 1213464576 | bytes 7086080 | tf_op jit(solution)/shard_map/dot_general | solution.py:49
  201.7 68.6 %grads_sum.1 = (f32[96,1536]{1,0:T(8,128)}, f32[96,768]{1,0:T(8,128)}, f32[16,1,1536]{2,1,0:T(1,128)}) custom-call(bf16[4,2,2,96,1536]{4,3,2,1,0:T(8,128)(2,1)} %bitcast.55, bf16[4,2,2,96,768]{4,3,2,1,0:T(8,128)(2,1)} %bitcast.59, f32[16,1,1536]{2,1,0:T(1,128)} %bitcast.63), custom_call_target="tpu_custom_call" | custom-call | tf_op jit(solution)/shard_map/grads_sum/pallas_call | solution.py:294
  270.3 2.3 reshape.283
  272.6 1.1 reduce.43
  273.7 0.7 slice.482
  274.4 1.7 copy.31
  (227 shorter events, 0.8 us)
Async XLA Ops:
  7.2 63.4 %copy-start = (bf16[128,16,320]{0,2,1:T(8,128)(2,1)S(1)}, bf16[128,16,320]{0,2,1:T(8,128)(2,1)}, u32[]{:S(2)}) copy-start(bf16[128,16,320]{0,2,1:T(8,128)(2,1)} %param.13) | copy-start | bytes 3932164
  7.2 57.6 %all-gather.5.cloned.1.call-start = ((), (), s32[]{:S(2)}) async-start(), calls=%async_computation.2 | async-start | bytes 5013504 | tf_op jit(solution)/shard_map/all_gather | solution.py:356
  7.9 82.0 %all-gather.9.cloned.1.call-start = ((), (), s32[]{:S(2)}) async-start(), calls=%async_computation.4 | async-start | bytes 2064384 | tf_op jit(solution)/shard_map/all_gather | solution.py:383
  10.9 123.1 %all-gather.7.cloned.1.call-start = ((), (), s32[]{:S(2)}) async-start(), calls=%async_computation.3 | async-start | bytes 2506752 | tf_op jit(solution)/shard_map/all_gather | solution.py:415
  64.7 5.5 %copy-start.88 = (s32[1,16]{1,0:T(1,128)S(1)}, s32[1,16]{1,0:T(1,128)}, u32[]{:S(2)}) copy-start(s32[1,16]{1,0:T(1,128)} %param.14) | copy-start | bytes 196
  64.7 5.5 %copy-start.89 = (s32[128]{0:T(128)S(1)}, s32[128]{0:T(128)}, u32[]{:S(2)}) copy-start(s32[128]{0:T(128)} %param.15) | copy-start | bytes 1540
  64.8 5.5 %copy-start.90 = (s32[128]{0:T(128)S(1)}, s32[128]{0:T(128)}, u32[]{:S(2)}) copy-start(s32[128]{0:T(128)} %param.16) | copy-start | bytes 1540
  70.2 5.7 %copy-start.87 = (f32[768]{0:T(1024)S(1)}, f32[768]{0:T(1024)}, u32[]{:S(2)}) copy-start(f32[768]{0:T(1024)} %param.19) | copy-start | bytes 9220
  70.2 10.1 %copy-start.10 = (f32[31,768]{1,0:T(8,128)S(1)}, f32[31,768]{1,0:T(8,128)}, u32[]{:S(2)}) copy-start(f32[31,768]{1,0:T(8,128)} %param.21) | copy-start | bytes 285700
  72.0 10.0 %all-to-all-start = ((bf16[16,16,322]{2,1,0:T(8,128)(2,1)}), bf16[16,16,322]{2,1,0:T(8,128)(2,1)S(1)}, u32[]{:S(2)}, u32[]{:S(2)}) async-start(bf16[16,16,322]{2,1,0:T(8,128)(2,1)} %copy.26), calls=%async_computation | async-start | bytes 393216 | tf_op jit(solution)/shard_map/all_to_all | solution.py:369
  92.0 4.5 %copy-start.6 = (f32[256,1536]{1,0:T(8,128)}, f32[256,1536]{1,0:T(8,128)S(1)}, u32[]{:S(2)}) copy-start(f32[256,1536]{1,0:T(8,128)S(1)} %get-tuple-element.104) | copy-start | bytes 4718596
  92.6 3.8 %copy-start.79 = (f32[256]{0:T(256)S(1)}, f32[256]{0:T(256)}, u32[]{:S(2)}) copy-start(f32[256]{0:T(256)} %copy-done.78) | copy-start | bytes 3076
  96.4 1.5 copy-start.16
  96.5 1.5 copy-start.18
  96.5 1.5 copy-start.20
  96.5 1.5 copy-start.22
  96.5 1.5 copy-start.24
  96.5 1.5 copy-start.26
  96.8 37.3 %copy-start.9 = (bf16[256,768]{1,0:T(8,128)(2,1)S(1)}, bf16[256,768]{1,0:T(8,128)(2,1)}, u32[]{:S(2)}) copy-start(bf16[256,768]{1,0:T(8,128)(2,1)} %param.25) | copy-start | bytes 1179652
  137.5 19.6 %all-to-all-start.1 = ((bf16[2,256,768]{1,2,0:T(8,128)(2,1)}), bf16[2,256,768]{1,2,0:T(8,128)(2,1)}, u32[]{:S(2)}, u32[]{:S(2)}) async-start(bf16[2,256,768]{1,2,0:T(8,128)(2,1)} %pad_maximum_fusion), calls=%async_computation.1 | async-start | bytes 1572864 | tf_op jit(solution)/shard_map/all_to_all | solution.py:420
  161.6 20.7 %copy-start.2 = (f32[256,768]{1,0:T(8,128)S(1)}, f32[256,768]{1,0:T(8,128)}, u32[]{:S(2)}) copy-start(f32[256,768]{1,0:T(8,128)} %copy-done.1) | copy-start | bytes 2359300
  161.6 20.8 %copy-start.3 = (f32[16,16,768]{2,1,0:T(8,128)S(1)}, f32[16,16,768]{2,1,0:T(8,128)}, u32[]{:S(2)}) copy-start(f32[16,16,768]{2,1,0:T(8,128)} %get-tuple-element.97) | copy-start | bytes 2359300
  161.6 20.8 %copy-start.12 = (f32[768]{0:T(1024)S(1)}, f32[768]{0:T(1024)}, u32[]{:S(2)}) copy-start(f32[768]{0:T(1024)} %copy-done.11) | copy-start | bytes 9220
  161.6 20.8 %copy-start.14 = (f32[768]{0:T(1024)S(1)}, f32[768]{0:T(1024)}, u32[]{:S(2)}) copy-start(f32[768]{0:T(1024)} %copy-done.13) | copy-start | bytes 9220
  161.6 20.8 %copy-start.15 = (f32[768]{0:T(1024)S(1)}, f32[768]{0:T(1024)}, u32[]{:S(2)}) copy-start(f32[768]{0:T(1024)} %param.22) | copy-start | bytes 9220
  163.6 21.9 %copy-start.80 = (f32[256]{0:T(256)S(1)}, f32[256]{0:T(256)}, u32[]{:S(2)}) copy-start(f32[256]{0:T(256)} %copy-done.78) | copy-start | bytes 3076
  182.3 4.7 %copy-start.82 = (f32[768]{0:T(1024)}, f32[768]{0:T(1024)S(1)}, u32[]{:S(2)}) copy-start(f32[768]{0:T(1024)S(1)} %get-tuple-element.117) | copy-start | bytes 9220
  185.2 1.8 copy-start.17
  185.2 1.8 copy-start.19
  185.2 1.8 copy-start.21
  185.2 1.8 copy-start.23
  185.2 1.8 copy-start.25
  185.2 1.8 copy-start.27
  185.3 1.8 copy-start.29
  185.3 1.8 copy-start.31
  185.3 1.8 copy-start.33
  185.3 1.8 copy-start.35
  185.3 1.8 copy-start.37
  185.3 1.8 copy-start.39
  185.3 1.8 copy-start.41
  185.3 1.8 copy-start.43
  185.3 1.8 copy-start.45
  185.3 1.8 copy-start.47
  185.4 1.8 copy-start.49
  185.4 1.8 copy-start.51
  185.4 1.8 copy-start.53
  185.4 1.8 copy-start.55
  185.4 1.8 copy-start.57
  185.4 1.8 copy-start.59
  185.4 1.8 copy-start.61
  185.4 1.8 copy-start.63
  185.4 1.8 copy-start.65
  185.5 1.8 copy-start.67
  185.5 1.8 copy-start.69
  185.5 1.8 copy-start.71
  185.5 1.8 copy-start.73
  185.5 1.8 copy-start.75
  185.5 1.8 copy-start.77
  185.5 5.1 %copy-start.8 = (bf16[256,1536]{1,0:T(8,128)(2,1)S(1)}, bf16[256,1536]{1,0:T(8,128)(2,1)}, u32[]{:S(2)}) copy-start(bf16[256,1536]{1,0:T(8,128)(2,1)} %get-tuple-element.13) | copy-start | bytes 2359300
  187.3 5.6 %copy-start.91 = (bf16[1536,768]{1,0:T(8,128)(2,1)S(1)}, bf16[1536,768]{1,0:T(8,128)(2,1)}, u32[]{:S(2)}) copy-start(bf16[1536,768]{1,0:T(8,128)(2,1)} %all-gather.7.cloned.1.call-done) | copy-start | bytes 7077892
  194.0 1.7 copy-start.81
  195.1 2.8 %copy-start.84 = (f32[256]{0:T(256)S(1)}, f32[256]{0:T(256)}, u32[]{:S(2)}) copy-start(f32[256]{0:T(256)} %copy-done.83) | copy-start | bytes 3076
  195.1 2.8 %copy-start.86 = (f32[256]{0:T(256)S(1)}, f32[256]{0:T(256)}, u32[]{:S(2)}) copy-start(f32[256]{0:T(256)} %copy-done.85) | copy-start | bytes 3076
  195.7 2.2 copy-start.7
  (33 other events, 43.7 us)
Sparse Core Ops, SparseCore 0:
  10.3 54.4 all-gather.4
  66.3 23.5 all-gather.8
  92.2 41.7 all-gather.6

commit v2 on v1

--- a/solution.py
+++ b/solution.py
@@ -336,6 +336,102 @@
     return o1, o2, ok.reshape(-1)[: gk.size].reshape(gk.shape)
 
 
+def spread_kernel(
+    n, w1, w2, pk, rt, gn, f1, f2, rec, rts, gns, z_sem, x_sem, core_sem, p_sem, r_sem, g_sem
+):
+    m = n // 4
+    me, mine = lax.axis_index("dp"), lax.axis_index("mp")
+    c = lax.rem(me, 2)
+    b = lax.rem(me // 2, 2)
+    a = me // 4
+    core_peer = me + 1 - 2 * c
+    x_peer = me + 2 - 4 * b
+    greet(("dp", "mp"))
+    small = push_all("dp", lambda peer: pk.at[peer], rec, p_sem.at[0], p_sem.at[1])
+    full = (f1, f2)
+    z, x, core = ({}, {}), ({}, {}), ({}, {})
+
+    def to_core(i, src, at, j):
+        core[i][j] = push(
+            src, full[i].at[at], core_sem.at[i, 0, j], core_sem.at[i, 1, j], "dp", core_peer
+        )
+
+    def to_x(i, src, at, k):
+        x[i][k] = push(src, full[i].at[at], x_sem.at[i, 0, k], x_sem.at[i, 1, k], "dp", x_peer)
+
+    for i, w in enumerate((w1, w2)):
+        for k in range(1, m):
+            peer = lax.rem(a + k, m) * 4 + b * 2 + c
+            z[i][k] = push(w, full[i].at[me], z_sem.at[i, 0, k], z_sem.at[i, 1, k], "dp", peer)
+        to_x(i, w, me, 0)
+        to_core(i, w, me, 0)
+    small += push_all("mp", lambda peer: rt, rts, r_sem.at[0], r_sem.at[1])
+    small += push_all("mp", lambda peer: gn, gns, g_sem.at[0], g_sem.at[1])
+    f1[me] = w1[...]
+    f2[me] = w2[...]
+    rec[me] = pk[me]
+    rts[mine] = rt[...]
+    gns[mine] = gn[...]
+
+    def z_step(i, k):
+        z[i][k].wait_recv()
+        at = lax.rem(a - k + m, m) * 4 + b * 2 + c
+        to_x(i, full[i].at[at], at, k)
+        to_core(i, full[i].at[at], at, k)
+
+    def x_step(i, k):
+        x[i][k].wait_recv()
+        at = lax.rem(a - k + m, m) * 4 + (1 - b) * 2 + c
+        to_core(i, full[i].at[at], at, m + k)
+
+    for k in range(1, m):
+        z_step(0, k)
+    x_step(0, 0)
+    for k in range(1, m):
+        z_step(1, k)
+        x_step(0, k)
+    for k in range(m):
+        x_step(1, k)
+    for copy in small:
+        copy.wait()
+    for i in range(2):
+        for copy in z[i].values():
+            copy.wait_send()
+        for copy in x[i].values():
+            copy.wait_send()
+        for copy in core[i].values():
+            copy.wait()
+
+
+def spread(w1, w2, packed, right, gain, cid):
+    n, q = lax.axis_size("dp"), lax.axis_size("mp")
+    m = n // 4
+    return pl.pallas_call(
+        functools.partial(spread_kernel, n),
+        out_shape=(
+            jax.ShapeDtypeStruct((n,) + w1.shape, BF16),
+            jax.ShapeDtypeStruct((n,) + w2.shape, BF16),
+            jax.ShapeDtypeStruct(packed.shape, BF16),
+            jax.ShapeDtypeStruct((q,) + right.shape, BF16),
+            jax.ShapeDtypeStruct((q,) + gain.shape, F32),
+        ),
+        in_specs=[VMEM] * 5,
+        out_specs=(VMEM,) * 5,
+        scratch_shapes=[
+            DMA((2, 2, m)),
+            DMA((2, 2, m)),
+            DMA((2, 2, 2 * m)),
+            DMA((2, n)),
+            DMA((2, q)),
+            DMA((2, q)),
+        ],
+        compiler_params=pltpu.CompilerParams(
+            collective_id=cid, has_side_effects=True, vmem_limit_bytes=LIMIT
+        ),
+        name="spread",
+    )(w1, w2, packed, right, gain)
+
+
 def on_device(
     corpus,
     picks,
@@ -353,8 +449,7 @@
 ):
     model_width = w_pw2.shape[0] * lax.axis_size("dp")
     parts = lax.axis_size("mp")
-    weights_one = lax.all_gather(w_pw1, "dp", axis=0, tiled=True).reshape(model_width, -1)
-    half = weights_one.shape[1] // 2
+    half = w_pw2.shape[1]
     feats = corpus.shape[2]
     frames = corpus.shape[1]
     picked = picks[0][:, None] == jnp.arange(corpus.shape[0], dtype=jnp.int32)[None, :]
@@ -365,8 +460,15 @@
     lang_send = jnp.sum(jnp.where(picked, langs[None, :], 0), 1)
     whole = jnp.stack([lens_send, lang_send], 1).astype(BF16)
     whole = jnp.broadcast_to(whole[:, None, :], (whole.shape[0], frames, 2))
-    packed = jnp.concatenate([blocks, whole], 2)
-    received = lax.all_to_all(packed, "dp", split_axis=0, concat_axis=0, tiled=True)
+    lanes = -(-(feats + 2) // 128) * 128
+    spare = jnp.zeros((whole.shape[0], frames, lanes - feats - 2), BF16)
+    packed = jnp.concatenate([blocks, whole, spare], 2)
+    right = jnp.concatenate([w_in, lang_table], 0)
+    weights_one, weights_two, received, right_full, gain_full = spread(
+        w_pw1.reshape(w_pw1.shape[0], -1), w_pw2, packed, right, ln_gain[None], 4
+    )
+    weights_one = weights_one.reshape(model_width, -1)
+    weights_two = weights_two.reshape(model_width, -1)
     lens = received[:, 0, feats].astype(jnp.int32)
     lang = received[:, 0, feats + 1].astype(jnp.int32)
     valid = (
@@ -379,11 +481,11 @@
     )
     onehot = jnp.repeat(onehot, frames, axis=0)
     left = jnp.concatenate([mel, onehot], 1)
-    right = jnp.concatenate([w_in, lang_table], 0)
-    right_full = lax.all_gather(right, "mp", axis=1, tiled=True)
-    gain_full = lax.all_gather(ln_gain, "mp", axis=0, tiled=True)
     inputs = jnp.dot(left, right, preferred_element_type=F32)
-    full_in = jnp.dot(left, right_full, preferred_element_type=F32)
+    full_in = jnp.concatenate(
+        [jnp.dot(left, right_full[p], preferred_element_type=F32) for p in range(parts)], 1
+    )
+    gain_full = gain_full.reshape(-1)
     mean = jnp.sum(full_in, 1) / model_width
     var = jnp.sum(full_in * full_in, 1) / model_width - mean * mean
     normed_full = (
@@ -411,8 +513,6 @@
     act = normed_conv * bn_gain + bn_bias
     act_sig = jax.nn.sigmoid(act)
     hidden = (valid_col * act * act_sig).astype(jnp.bfloat16)
-    w_later, _ = lax.optimization_barrier((w_pw2, weights_one))
-    weights_two = lax.all_gather(w_later, "dp", axis=0, tiled=True)
     partial = lax.dot_general(
         cotangent, weights_two, (((1,), (1,)), ((), ())), preferred_element_type=F32
     ).astype(BF16)

time: 284 us -> 242 us (0.85)
  waiting for transfers between devices: 92.6 us -> 0.01 us
  Pallas kernels: 93 us -> 164 us
  between operations: 15.3 us -> 2.25 us
  matrix products: 16.9 us -> 24 us
  local copies, waits for them, and re-layouts: 24.4 us -> 18.1 us
  blocking collectives: 4.38 us -> 0 us
  starting transfers between devices: 8.28 us -> 4.34 us
    all_gather x3 -> x0, waiting for transfers between devices: 91.6 us -> none  [the longest x1 53.8 us: on_device(): lax.all_gather(w_pw1, 'dp', axis=0, tiled=True).reshape(model_width, -1)]
    pallas_call x0 -> x1, Pallas kernels: none -> 64.4 us  [spread(): pl.pallas_call(functools.partial(spread_kernel, n), out_shape=(jax.ShapeD...]
    unnamed x189 -> x179, local copies, waits for them, and re-layouts: 11.9 us -> 5.23 us
    pallas_call x1, Pallas kernels: 8.14 us -> 14.5 us  [stats_sum(): pl.pallas_call(stats_kernel, out_shape=jax.ShapeDtypeStruct(row.shape, F3...]
    all_gather x1 -> x0, blocking collectives: 4.38 us -> none  [on_device(): gain_full = lax.all_gather(ln_gain, 'mp', axis=0, tiled=True)]
    all_to_all x1 -> x0, starting transfers between devices: 3.85 us -> none  [on_device(): lax.all_to_all(packed, 'dp', split_axis=0, concat_axis=0, tiled=True)]
  transfers between devices with their start and end apart: 5 -> 1, of which waited for: 4 -> 0; matrix products, arithmetic and copies ran while one was open for 10% -> 10% of each run, Pallas kernels for 3% -> 6%
where the time goes in v2:
time: 242 us; the launch traced here: 241 us
  Pallas kernels  164 us (68%)
  other arithmetic  28.2 us (12%)
  matrix products  24 us (10%)
  local copies, waits for them, and re-layouts  18.1 us (7%)
  starting transfers between devices  4.34 us (2%)
    pallas_call x1, Pallas kernels, grads_sum(): pl.pallas_call(functools.partial(grads_kernel, n), out_shape=(jax.ShapeDt...  67.8 us
    pallas_call x1, Pallas kernels, spread(): pl.pallas_call(functools.partial(spread_kernel, n), out_shape=(jax.ShapeD...  64.4 us
    pallas_call x1, Pallas kernels, stats_hidden(): pl.pallas_call(stats_hidden_kernel, out_shape=(jax.ShapeDtypeStruct(row.s...  17.6 us
    pallas_call x1, Pallas kernels, stats_sum(): pl.pallas_call(stats_kernel, out_shape=jax.ShapeDtypeStruct(row.shape, F3...  14.5 us
    dot_general x2, matrix products, contract_rows(): lax.dot_general(left, right, (((0,), (0,)), ((), ())), preferred_element_...  7.46 us
    unnamed x179, local copies, waits for them, and re-layouts  5.23 us
  transfers between devices with their start and end apart: 1, of which 0 were waited for; matrix products, arithmetic and copies ran while one was open for 10% of the time, Pallas kernels for 6%

profile of v2, /device:TPU:8, one launch (start us, length us, event | category | flops | bytes accessed | tf_op | source)
XLA Modules:
  0.0 241.3 jit_solution(8611459162721445117)
XLA Ops:
  0.6 0.0 copy-start
  0.7 1.8 copy.29
  2.5 0.9 select_reduce_fusion.1
  3.4 0.1 copy.27
  3.5 1.3 fusion.79
  5.0 0.6 broadcast_in_dim.63.gn
  5.6 0.1 pad.30.clone
  5.7 0.9 maximum_maximum_fusion.pk
  6.6 64.4 %spread.1 = (bf16[16,96,1536]{2,1,0:T(8,128)(2,1)}, bf16[16,96,768]{2,1,0:T(8,128)(2,1)}, bf16[16,16,384]{2,1,0:T(8,128)(2,1)}, bf16[2,448,768]{2,1,0:T(8,128)(2,1)}, f32[2,1,768]{2,1,0:T(1,128)}) custom-call(bf16[96,1536]{1,0:T(8,128)(2,1)} %bitcast.71, bf16[96,768]{1,0:T(8,128)(2,1)} %w2.1, bf16[16,16,384]{2,1,0:T(8,128)(2,1)} %maximum_maximum_fusion.pk, ...), custom_call_target="tpu_custom_call" | custom-call | tf_op jit(solution)/shard_map/spread/pallas_call | solution.py:409
  71.0 2.5 %fusion = bf16[256,1536]{0,1:T(8,128)(2,1)S(1)} fusion(bf16[1536,768]{1,0:T(8,128)(2,1)} %bitcast.82, bf16[256,768]{1,0:T(8,128)(2,1)S(1)} %copy-done.10), kind=kOutput, calls=%fused_computation.63 | convolution fusion | flops 604372992 | bytes 3538944 | tf_op jit(solution)/shard_map/dot_general | solution.py:516
  73.5 0.0 copy-start.13
  73.5 0.1 slice_bitcast_fusion.1
  73.6 1.0 pad_maximum_fusion.1
  74.5 4.3 %all-to-all-start = ((bf16[2,256,768]{1,2,0:T(8,128)(2,1)}), bf16[2,256,768]{1,2,0:T(8,128)(2,1)}, u32[]{:S(2)}, u32[]{:S(2)}) async-start(bf16[2,256,768]{1,2,0:T(8,128)(2,1)} %pad_maximum_fusion.1), calls=%async_computation | async-start | bytes 1572864 | tf_op jit(solution)/shard_map/all_to_all | solution.py:520
  78.9 0.7 convert_reduce_fusion.2
  79.6 0.7 fusion.84
  80.3 0.1 fusion.81
  80.4 0.7 slice_reduce_fusion.30
  81.1 0.7 slice_reduce_fusion.31
  81.8 0.1 fusion.82
  81.9 0.1 reshape.298
  82.0 0.1 bitcast_multiply_fusion.1
  82.1 0.4 copy-done.77
  82.5 2.1 fusion.93
  84.7 2.4 %fusion.92 = (f32[256]{0:T(256)}, f32[256,768]{1,0:T(8,128)S(1)}) fusion(bf16[2,448,768]{2,1,0:T(8,128)(2,1)} %get-tuple-element.18, bf16[256,128]{1,0:T(8,128)(2,1)S(1)} %bitcast.75, bf16[256,320]{1,0:T(8,128)(2,1)S(1)} %bitcast_multiply_fusion.1), kind=kOutput, calls=%fused_computation.264 | convolution fusion | flops 176815872 | bytes 1704960 | tf_op jit(solution)/shard_map/dot_general | solution.py:486
  87.1 1.3 reduce.10
  88.4 1.3 mul.794
  89.7 0.2 multiply_reduce_fusion
  89.9 0.7 add_rsqrt_fusion
  90.6 4.3 %fusion.89 = f32[256,1536]{1,0:T(8,128)S(1)} fusion(bf16[1536,1536]{1,0:T(8,128)(2,1)} %bitcast.81, f32[256,768]{1,0:T(8,128)} %copy-done.7, f32[256,768]{1,0:T(8,128)} %copy-done.8, f32[1536]{0:T(1024)} %mul.794, f32[256]{0:T(256)S(1)} %get-tuple-element.104, f32[256]{0:T(256)S(1)} %get-tuple-element.105), kind=kOutput, calls=%fused_computation.261 | convolution fusion | flops 1209925632 | bytes 7872512 | tf_op jit(solution)/shard_map/dot_general | solution.py:494
  95.1 0.0 copy-start.53
  95.2 0.2 multiply_multiply_fusion.1
  95.5 0.9 copy-done.1
  96.6 3.6 %multiply_reduce_fusion.1 = (f32[768]{0:T(1024)S(1)}, f32[768]{0:T(1024)S(1)}, f32[16,16,768]{2,1,0:T(8,128)}) fusion(f32[16,16]{1,0:T(8,128)S(1)} %fusion.81, f32[768]{0:T(1024)S(1)} %copy-done.73, f32[768]{0:T(1024)S(1)} %copy-done.75, f32[768]{0:T(1024)S(1)} %get-tuple-element.64, f32[768]{0:T(1024)S(1)} %copy-done.19, f32[768]{0:T(1024)S(1)} %copy-done.21, ...), kind=kLoop, calls=%fused_computation.71 | loop fusion | flops 12777984 | bytes 1675264 | tf_op jit(solution)/shard_map/reduce_sum | solution.py:502
  100.3 0.6 broadcast_in_dim.65
  101.0 0.6 broadcast_in_dim.66.x_ref
  101.6 14.5 %stats_sum.1 = f32[1,1664]{1,0:T(1,128)} custom-call(f32[1,1664]{1,0:T(1,128)} %broadcast_in_dim.66.x_ref), custom_call_target="tpu_custom_call" | custom-call | tf_op jit(solution)/shard_map/stats_sum/pallas_call | solution.py:116
  116.1 1.2 slice.456
  117.3 1.3 fusion.91
  118.5 2.2 multiply_convert_fusion.3.h_ref
  120.7 0.0 all-to-all-done
  120.7 2.2 convert_reduce_fusion
  122.9 2.3 copy.28
  125.2 1.9 fusion.90
  127.1 0.6 broadcast_in_dim.67.x_ref
  127.7 17.6 %stats_hidden.1 = (f32[1,1536]{1,0:T(1,128)}, bf16[256,1536]{1,0:T(8,128)(2,1)}) custom-call(f32[1,1536]{1,0:T(1,128)} %broadcast_in_dim.67.x_ref, bf16[256,768]{1,0:T(8,128)(2,1)} %multiply_convert_fusion.3.h_ref), custom_call_target="tpu_custom_call" | custom-call | tf_op jit(solution)/shard_map/stats_hidden/pallas_call | solution.py:150
  145.3 2.7 %fusion.94 = f32[256,768]{1,0:T(8,128)S(1)} fusion(bf16[256,1536]{1,0:T(8,128)(2,1)} %get-tuple-element.21, bf16[1536,768]{1,0:T(8,128)(2,1)} %bitcast.83), kind=kOutput, calls=%fused_computation.266 | convolution fusion | flops 603979776 | bytes 3932160 | tf_op jit(solution)/shard_map/dot_general | solution.py:526
  148.1 0.0 copy-start.14
  148.1 2.3 convolution_convert_fusion.1
  150.6 0.0 copy-start.54
  150.7 1.2 slice_reduce_fusion.32
  151.9 2.6 %multiply_reduce_fusion.2 = (f32[768]{0:T(1024)S(1)}, f32[768]{0:T(1024)S(1)}, f32[768]{0:T(1024)S(1)}, f32[768]{0:T(1024)S(1)}, f32[768]{0:T(1024)S(1)}, /*inde...) fusion(f32[16,16,768]{2,1,0:T(8,128)S(1)} %bitcast.67, ...), kind=kLoop, calls=%fused_computation.146 | loop fusion | flops 8833536 | bytes 3217412 | tf_op jit(solution)/shard_map/reduce_sum | solution.py:44
  154.9 2.5 %fusion.54 = f32[16,16,768]{2,1,0:T(8,128)S(1)} fusion(f32[16,16,768]{2,1,0:T(8,128)S(1)} %get-tuple-element.101, f32[768]{0:T(1024)S(1)} %copy-done.74, f32[768]{0:T(1024)S(1)} %copy-done.76, f32[768]{0:T(1024)S(1)} %copy-done.18, f32[768]{0:T(1024)S(1)} %copy-done.20, f32[768]{0:T(1024)S(1)} %copy-done.22, f32[768]{0:T(1024)S(1)} %copy-done.24, ...), kind=kLoop, calls=%fused_computation.124 | loop fusion | flops 11993088 | bytes 1668096 | tf_op jit(solution)/shard_map/add | solution.py:32
  157.4 1.7 multiply_reduce_fusion.21
  159.1 1.1 fusion.1
  160.2 1.1 multiply_convert_fusion.2
  161.7 0.2 stack.151
  161.9 5.2 %convolution_convert_fusion = bf16[1536,1536]{1,0:T(8,128)(2,1)} fusion(bf16[256,768]{1,0:T(8,128)(2,1)} %get-tuple-element.107, bf16[256,768]{1,0:T(8,128)(2,1)S(1)} %get-tuple-element.106, f32[256,768]{1,0:T(8,128)} %copy-done.7, f32[256,768]{1,0:T(8,128)} %copy-done.8, f32[1536]{0:T(1024)S(1)} %copy-done.81, f32[256]{0:T(256)S(1)} %copy-done.85, ...), kind=kOutput, calls=%fused_computation.60 | convolution fusion | flops 1213857792 | bytes 7086080 | tf_op jit(solution)/shard_map/dot_general | solution.py:49
  167.1 0.6 pad.14
  167.7 67.8 %grads_sum.1 = (f32[96,1536]{1,0:T(8,128)}, f32[96,768]{1,0:T(8,128)}, f32[16,1,1536]{2,1,0:T(1,128)}) custom-call(bf16[4,2,2,96,1536]{4,3,2,1,0:T(8,128)(2,1)} %bitcast.70, bf16[4,2,2,96,768]{4,3,2,1,0:T(8,128)(2,1)} %bitcast.69, f32[16,1,1536]{2,1,0:T(1,128)} %bitcast.72), custom_call_target="tpu_custom_call" | custom-call | tf_op jit(solution)/shard_map/grads_sum/pallas_call | solution.py:294
  235.6 2.3 reshape.296
  237.8 1.1 reduce.45
  238.9 0.7 slice.490
  239.6 1.7 copy.34
  (212 shorter events, 0.6 us)
Async XLA Ops:
  0.6 2.9 %copy-start = (bf16[128,16,320]{0,2,1:T(8,128)(2,1)S(1)}, bf16[128,16,320]{0,2,1:T(8,128)(2,1)}, u32[]{:S(2)}) copy-start(bf16[128,16,320]{0,2,1:T(8,128)(2,1)} %param.13) | copy-start | bytes 3932164
  0.6 4.3 %copy-start.9 = (bf16[320,768]{1,0:T(8,128)(2,1)S(1)}, bf16[320,768]{1,0:T(8,128)(2,1)}, u32[]{:S(2)}) copy-start(bf16[320,768]{1,0:T(8,128)(2,1)} %param.17) | copy-start | bytes 1474564
  0.7 4.3 %copy-start.83 = (f32[768]{0:T(1024)S(1)}, f32[768]{0:T(1024)}, u32[]{:S(2)}) copy-start(f32[768]{0:T(1024)} %param.19) | copy-start | bytes 9220
  0.7 5.0 %copy-start.12 = (bf16[128,768]{1,0:T(8,128)(2,1)S(1)}, bf16[128,768]{1,0:T(8,128)(2,1)}, u32[]{:S(2)}) copy-start(bf16[128,768]{1,0:T(8,128)(2,1)} %param.18) | copy-start | bytes 589828
  3.5 67.5 %copy-start.10 = (bf16[256,768]{1,0:T(8,128)(2,1)S(1)}, bf16[256,768]{1,0:T(8,128)(2,1)}, u32[]{:S(2)}) copy-start(bf16[256,768]{1,0:T(8,128)(2,1)} %param.25) | copy-start | bytes 1179652
  73.5 5.4 %copy-start.11 = (bf16[16,16,384]{2,1,0:T(8,128)(2,1)S(1)}, bf16[16,16,384]{2,1,0:T(8,128)(2,1)}, u32[]{:S(2)}) copy-start(bf16[16,16,384]{2,1,0:T(8,128)(2,1)} %get-tuple-element.16) | copy-start | bytes 589828
  73.5 6.9 %copy-start.13 = (f32[31,768]{1,0:T(8,128)S(1)}, f32[31,768]{1,0:T(8,128)}, u32[]{:S(2)}) copy-start(f32[31,768]{1,0:T(8,128)} %param.21) | copy-start | bytes 285700
  74.5 46.2 %all-to-all-start = ((bf16[2,256,768]{1,2,0:T(8,128)(2,1)}), bf16[2,256,768]{1,2,0:T(8,128)(2,1)}, u32[]{:S(2)}, u32[]{:S(2)}) async-start(bf16[2,256,768]{1,2,0:T(8,128)(2,1)} %pad_maximum_fusion.1), calls=%async_computation | async-start | bytes 1572864 | tf_op jit(solution)/shard_map/all_to_all | solution.py:520
  81.8 13.7 %copy-start.15 = (f32[768]{0:T(1024)}, f32[768]{0:T(1024)S(1)}, u32[]{:S(2)}) copy-start(f32[768]{0:T(1024)S(1)} %get-tuple-element.63) | copy-start | bytes 9220
  81.8 13.7 %copy-start.17 = (f32[768]{0:T(1024)}, f32[768]{0:T(1024)S(1)}, u32[]{:S(2)}) copy-start(f32[768]{0:T(1024)S(1)} %get-tuple-element.64) | copy-start | bytes 9220
  84.7 5.9 %copy-start.7 = (f32[256,768]{1,0:T(8,128)}, f32[256,768]{1,0:T(8,128)S(1)}, u32[]{:S(2)}) copy-start(f32[256,768]{1,0:T(8,128)S(1)} %get-tuple-element.113) | copy-start | bytes 2359300
  87.1 3.5 %copy-start.8 = (f32[256,768]{1,0:T(8,128)}, f32[256,768]{1,0:T(8,128)S(1)}, u32[]{:S(2)}) copy-start(f32[256,768]{1,0:T(8,128)S(1)} %get-tuple-element.111) | copy-start | bytes 2359300
  90.6 4.3 %copy-start.84 = (f32[256]{0:T(256)}, f32[256]{0:T(256)S(1)}, u32[]{:S(2)}) copy-start(f32[256]{0:T(256)S(1)} %get-tuple-element.104) | copy-start | bytes 3076
  90.6 4.3 %copy-start.86 = (f32[256]{0:T(256)}, f32[256]{0:T(256)S(1)}, u32[]{:S(2)}) copy-start(f32[256]{0:T(256)S(1)} %get-tuple-element.105) | copy-start | bytes 3076
  90.6 4.3 %copy-start.78 = (f32[256]{0:T(256)S(1)}, f32[256]{0:T(256)}, u32[]{:S(2)}) copy-start(f32[256]{0:T(256)} %copy-done.77) | copy-start | bytes 3076
  95.0 1.4 copy-start.19
  95.0 1.4 copy-start.21
  95.0 1.4 copy-start.23
  95.0 1.4 copy-start.25
  95.0 1.4 copy-start.27
  95.0 1.4 copy-start.29
  95.0 1.4 copy-start.31
  145.3 2.8 %copy-start.6 = (bf16[256,1536]{1,0:T(8,128)(2,1)S(1)}, bf16[256,1536]{1,0:T(8,128)(2,1)}, u32[]{:S(2)}) copy-start(bf16[256,1536]{1,0:T(8,128)(2,1)} %get-tuple-element.21) | copy-start | bytes 2359300
  148.1 2.6 %copy-start.82 = (f32[1,1536]{1,0:T(1,128)S(1)}, f32[1,1536]{1,0:T(1,128)}, u32[]{:S(2)}) copy-start(f32[1,1536]{1,0:T(1,128)} %get-tuple-element.22) | copy-start | bytes 18436
  148.1 3.8 %copy-start.2 = (f32[256,768]{1,0:T(8,128)S(1)}, f32[256,768]{1,0:T(8,128)}, u32[]{:S(2)}) copy-start(f32[256,768]{1,0:T(8,128)} %copy-done.1) | copy-start | bytes 2359300
  148.1 3.8 %copy-start.3 = (f32[16,16,768]{2,1,0:T(8,128)S(1)}, f32[16,16,768]{2,1,0:T(8,128)}, u32[]{:S(2)}) copy-start(f32[16,16,768]{2,1,0:T(8,128)} %get-tuple-element.103) | copy-start | bytes 2359300
  148.1 3.7 %copy-start.14 = (f32[768]{0:T(1024)S(1)}, f32[768]{0:T(1024)}, u32[]{:S(2)}) copy-start(f32[768]{0:T(1024)} %param.22) | copy-start | bytes 9220
  150.4 4.1 %copy-start.16 = (f32[768]{0:T(1024)S(1)}, f32[768]{0:T(1024)}, u32[]{:S(2)}) copy-start(f32[768]{0:T(1024)} %copy-done.15) | copy-start | bytes 9220
  150.4 4.1 %copy-start.18 = (f32[768]{0:T(1024)S(1)}, f32[768]{0:T(1024)}, u32[]{:S(2)}) copy-start(f32[768]{0:T(1024)} %copy-done.17) | copy-start | bytes 9220
  150.4 4.1 %copy-start.20 = (f32[768]{0:T(1024)S(1)}, f32[768]{0:T(1024)}, u32[]{:S(2)}) copy-start(f32[768]{0:T(1024)} %get-tuple-element.65) | copy-start | bytes 9220
  150.4 4.1 %copy-start.22 = (f32[768]{0:T(1024)S(1)}, f32[768]{0:T(1024)}, u32[]{:S(2)}) copy-start(f32[768]{0:T(1024)} %get-tuple-element.66) | copy-start | bytes 9220
  150.4 4.1 %copy-start.24 = (f32[768]{0:T(1024)S(1)}, f32[768]{0:T(1024)}, u32[]{:S(2)}) copy-start(f32[768]{0:T(1024)} %get-tuple-element.67) | copy-start | bytes 9220
  150.4 4.1 %copy-start.26 = (f32[768]{0:T(1024)S(1)}, f32[768]{0:T(1024)}, u32[]{:S(2)}) copy-start(f32[768]{0:T(1024)} %get-tuple-element.68) | copy-start | bytes 9220
  150.5 4.1 %copy-start.28 = (f32[768]{0:T(1024)S(1)}, f32[768]{0:T(1024)}, u32[]{:S(2)}) copy-start(f32[768]{0:T(1024)} %get-tuple-element.69) | copy-start | bytes 9220
  150.5 4.1 %copy-start.30 = (f32[768]{0:T(1024)S(1)}, f32[768]{0:T(1024)}, u32[]{:S(2)}) copy-start(f32[768]{0:T(1024)} %get-tuple-element.70) | copy-start | bytes 9220
  150.5 4.1 %copy-start.32 = (f32[768]{0:T(1024)S(1)}, f32[768]{0:T(1024)}, u32[]{:S(2)}) copy-start(f32[768]{0:T(1024)} %get-tuple-element.71) | copy-start | bytes 9220
  150.5 4.1 %copy-start.34 = (f32[768]{0:T(1024)S(1)}, f32[768]{0:T(1024)}, u32[]{:S(2)}) copy-start(f32[768]{0:T(1024)} %get-tuple-element.72) | copy-start | bytes 9220
  150.5 4.1 %copy-start.36 = (f32[768]{0:T(1024)S(1)}, f32[768]{0:T(1024)}, u32[]{:S(2)}) copy-start(f32[768]{0:T(1024)} %get-tuple-element.73) | copy-start | bytes 9220
  150.5 4.1 %copy-start.38 = (f32[768]{0:T(1024)S(1)}, f32[768]{0:T(1024)}, u32[]{:S(2)}) copy-start(f32[768]{0:T(1024)} %get-tuple-element.74) | copy-start | bytes 9220
  150.5 4.1 %copy-start.40 = (f32[768]{0:T(1024)S(1)}, f32[768]{0:T(1024)}, u32[]{:S(2)}) copy-start(f32[768]{0:T(1024)} %get-tuple-element.75) | copy-start | bytes 9220
  150.5 4.1 %copy-start.42 = (f32[768]{0:T(1024)S(1)}, f32[768]{0:T(1024)}, u32[]{:S(2)}) copy-start(f32[768]{0:T(1024)} %get-tuple-element.76) | copy-start | bytes 9220
  150.5 4.1 %copy-start.44 = (f32[768]{0:T(1024)S(1)}, f32[768]{0:T(1024)}, u32[]{:S(2)}) copy-start(f32[768]{0:T(1024)} %get-tuple-element.77) | copy-start | bytes 9220
  150.5 4.1 %copy-start.46 = (f32[768]{0:T(1024)S(1)}, f32[768]{0:T(1024)}, u32[]{:S(2)}) copy-start(f32[768]{0:T(1024)} %get-tuple-element.78) | copy-start | bytes 9220
  150.6 4.1 %copy-start.48 = (f32[768]{0:T(1024)S(1)}, f32[768]{0:T(1024)}, u32[]{:S(2)}) copy-start(f32[768]{0:T(1024)} %get-tuple-element.79) | copy-start | bytes 9220
  150.6 4.1 %copy-start.50 = (f32[768]{0:T(1024)S(1)}, f32[768]{0:T(1024)}, u32[]{:S(2)}) copy-start(f32[768]{0:T(1024)} %get-tuple-element.80) | copy-start | bytes 9220
  150.6 4.1 %copy-start.52 = (f32[768]{0:T(1024)S(1)}, f32[768]{0:T(1024)}, u32[]{:S(2)}) copy-start(f32[768]{0:T(1024)} %get-tuple-element.81) | copy-start | bytes 9220
  150.6 4.1 %copy-start.54 = (f32[768]{0:T(1024)S(1)}, f32[768]{0:T(1024)}, u32[]{:S(2)}) copy-start(f32[768]{0:T(1024)} %get-tuple-element.82) | copy-start | bytes 9220
  150.6 4.1 %copy-start.56 = (f32[768]{0:T(1024)S(1)}, f32[768]{0:T(1024)}, u32[]{:S(2)}) copy-start(f32[768]{0:T(1024)} %get-tuple-element.83) | copy-start | bytes 9220
  150.6 4.1 %copy-start.58 = (f32[768]{0:T(1024)S(1)}, f32[768]{0:T(1024)}, u32[]{:S(2)}) copy-start(f32[768]{0:T(1024)} %get-tuple-element.84) | copy-start | bytes 9220
  150.6 4.1 %copy-start.60 = (f32[768]{0:T(1024)S(1)}, f32[768]{0:T(1024)}, u32[]{:S(2)}) copy-start(f32[768]{0:T(1024)} %get-tuple-element.85) | copy-start | bytes 9220
  150.6 4.1 %copy-start.62 = (f32[768]{0:T(1024)S(1)}, f32[768]{0:T(1024)}, u32[]{:S(2)}) copy-start(f32[768]{0:T(1024)} %get-tuple-element.86) | copy-start | bytes 9220
  150.6 4.1 %copy-start.64 = (f32[768]{0:T(1024)S(1)}, f32[768]{0:T(1024)}, u32[]{:S(2)}) copy-start(f32[768]{0:T(1024)} %get-tuple-element.87) | copy-start | bytes 9220
  150.7 4.1 %copy-start.66 = (f32[768]{0:T(1024)S(1)}, f32[768]{0:T(1024)}, u32[]{:S(2)}) copy-start(f32[768]{0:T(1024)} %get-tuple-element.88) | copy-start | bytes 9220
  150.7 4.1 %copy-start.68 = (f32[768]{0:T(1024)S(1)}, f32[768]{0:T(1024)}, u32[]{:S(2)}) copy-start(f32[768]{0:T(1024)} %get-tuple-element.89) | copy-start | bytes 9220
  150.7 4.1 %copy-start.70 = (f32[768]{0:T(1024)S(1)}, f32[768]{0:T(1024)}, u32[]{:S(2)}) copy-start(f32[768]{0:T(1024)} %get-tuple-element.90) | copy-start | bytes 9220
  150.7 4.1 %copy-start.72 = (f32[768]{0:T(1024)S(1)}, f32[768]{0:T(1024)}, u32[]{:S(2)}) copy-start(f32[768]{0:T(1024)} %get-tuple-element.91) | copy-start | bytes 9220
  150.7 4.1 %copy-start.74 = (f32[768]{0:T(1024)S(1)}, f32[768]{0:T(1024)}, u32[]{:S(2)}) copy-start(f32[768]{0:T(1024)} %get-tuple-element.92) | copy-start | bytes 9220
  150.7 4.1 %copy-start.76 = (f32[768]{0:T(1024)S(1)}, f32[768]{0:T(1024)}, u32[]{:S(2)}) copy-start(f32[768]{0:T(1024)} %get-tuple-element.93) | copy-start | bytes 9220
  151.9 5.5 %copy-start.80 = (f32[768]{0:T(1024)}, f32[768]{0:T(1024)S(1)}, u32[]{:S(2)}) copy-start(f32[768]{0:T(1024)S(1)} %get-tuple-element.126) | copy-start | bytes 9220
  151.9 5.5 %copy-start.79 = (f32[256]{0:T(256)S(1)}, f32[256]{0:T(256)}, u32[]{:S(2)}) copy-start(f32[256]{0:T(256)} %copy-done.77) | copy-start | bytes 3076
  154.8 4.2 %copy-start.5 = (bf16[448,768]{1,0:T(8,128)(2,1)S(1)}, bf16[448,768]{1,0:T(8,128)(2,1)}, u32[]{:S(2)}) copy-start(bf16[448,768]{1,0:T(8,128)(2,1)} %copy-done.4) | copy-start | bytes 2064388
  160.2 1.6 copy-start.81
  160.2 1.7 copy-start.85
  160.2 1.7 copy-start.87
  (25 other events, 33.3 us)

commit v3 on v2

--- a/solution.py
+++ b/solution.py
@@ -122,52 +122,6 @@
         compiler_params=pltpu.CompilerParams(collective_id=cid, has_side_effects=True),
         name="stats_sum",
     )(row)
-
-
-def stats_hidden_kernel(
-    x_ref, h_ref, o_ref, hid_ref, slots, hslots, send, recv, hsend, hrecv
-):
-    size, me = lax.axis_size("dp"), lax.axis_index("dp")
-    parts, mine = lax.axis_size("mp"), lax.axis_index("mp")
-    chans = h_ref.shape[1]
-    greet(("dp", "mp"))
-    copies = push_all("dp", lambda peer: x_ref, slots, send, recv)
-    wide = push_all("mp", lambda peer: h_ref, hslots, hsend, hrecv)
-    slots[me] = x_ref[...]
-    hslots[mine] = h_ref[...]
-    for copy in copies:
-        copy.wait()
-    o_ref[...] = sum_slots(slots, size)
-    for copy in wide:
-        copy.wait()
-    for p in range(parts):
-        hid_ref[:, p * chans : (p + 1) * chans] = hslots[p]
-
-
-def stats_hidden(row, hidden, cid):
-    n, q = lax.axis_size("dp"), lax.axis_size("mp")
-    rows, chans = hidden.shape
-    return pl.pallas_call(
-        stats_hidden_kernel,
-        out_shape=(
-            jax.ShapeDtypeStruct(row.shape, F32),
-            jax.ShapeDtypeStruct((rows, q * chans), BF16),
-        ),
-        in_specs=[VMEM, VMEM],
-        out_specs=(VMEM, VMEM),
-        scratch_shapes=[
-            pltpu.VMEM((n,) + row.shape, F32),
-            pltpu.VMEM((q,) + hidden.shape, BF16),
-            DMA((n,)),
-            DMA((n,)),
-            DMA((q,)),
-            DMA((q,)),
-        ],
-        compiler_params=pltpu.CompilerParams(
-            collective_id=cid, has_side_effects=True, vmem_limit_bytes=LIMIT
-        ),
-        name="stats_hidden",
-    )(row, hidden)
 
 
 def grads_kernel(
@@ -348,59 +302,125 @@
     x_peer = me + 2 - 4 * b
     greet(("dp", "mp"))
     small = push_all("dp", lambda peer: pk.at[peer], rec, p_sem.at[0], p_sem.at[1])
-    full = (f1, f2)
-    z, x, core = ({}, {}), ({}, {}), ({}, {})
-
-    def to_core(i, src, at, j):
-        core[i][j] = push(
-            src, full[i].at[at], core_sem.at[i, 0, j], core_sem.at[i, 1, j], "dp", core_peer
-        )
-
-    def to_x(i, src, at, k):
-        x[i][k] = push(src, full[i].at[at], x_sem.at[i, 0, k], x_sem.at[i, 1, k], "dp", x_peer)
-
-    for i, w in enumerate((w1, w2)):
-        for k in range(1, m):
-            peer = lax.rem(a + k, m) * 4 + b * 2 + c
-            z[i][k] = push(w, full[i].at[me], z_sem.at[i, 0, k], z_sem.at[i, 1, k], "dp", peer)
-        to_x(i, w, me, 0)
-        to_core(i, w, me, 0)
     small += push_all("mp", lambda peer: rt, rts, r_sem.at[0], r_sem.at[1])
     small += push_all("mp", lambda peer: gn, gns, g_sem.at[0], g_sem.at[1])
+    owns, full = (w1, w2), (f1, f2)
+
+    def spot(line, row):
+        return line * 4 + row * 2 + c
+
+    def copy_of(src, i, at, sems, index, peer):
+        return pltpu.make_async_remote_copy(
+            src_ref=src,
+            dst_ref=full[i].at[at],
+            send_sem=sems.at[i, 0, index],
+            recv_sem=sems.at[i, 1, index],
+            device_id={"dp": peer},
+            device_id_type=MESH,
+        )
+
+    def has(way, k):
+        return a >= k if way == 0 else a + k < m
+
+    def source(way, k):
+        return a - k if way == 0 else a + k
+
+    def passes(way):
+        return a + 1 < m if way == 0 else a >= 1
+
+    def z_copy(i, src, at, way, hop):
+        peer = spot(a + 1, b) if way == 0 else spot(a - 1, b)
+        return copy_of(src, i, at, z_sem, way * m + hop, peer)
+
+    def x_copy(i, src, at, index):
+        return copy_of(src, i, at, x_sem, index, x_peer)
+
+    def core_copy(i, src, at, index):
+        return copy_of(src, i, at, core_sem, index, core_peer)
+
+    def begin(i):
+        for way in range(2):
+
+            @pl.when(passes(way))
+            def _():
+                z_copy(i, owns[i], me, way, 1).start()
+
+        x_copy(i, owns[i], me, 0).start()
+        core_copy(i, owns[i], me, 0).start()
+
+    def z_step(i, k, way):
+        @pl.when(has(way, k))
+        def _():
+            at = spot(source(way, k), b)
+            block = full[i].at[at]
+            z_copy(i, owns[i], me, way, k).wait_recv()
+            if k < m - 1:
+
+                @pl.when(passes(way))
+                def _():
+                    z_copy(i, block, at, way, k + 1).start()
+
+            x_copy(i, block, at, way * m + k).start()
+            core_copy(i, block, at, way * m + k).start()
+
+    def x_step(i, k, way):
+        @pl.when(has(way, k))
+        def _():
+            at = spot(source(way, k), 1 - b)
+            x_copy(i, owns[i], me, way * m + k).wait_recv()
+            core_copy(i, full[i].at[at], at, (2 + way) * m + k).start()
+
+    def finish(i):
+        for way in range(2):
+
+            @pl.when(passes(way))
+            def _():
+                z_copy(i, owns[i], me, way, 1).wait_send()
+
+        for k in range(m):
+            for way in range(2 if k else 1):
+
+                @pl.when(has(way, k))
+                def _():
+                    if 0 < k < m - 1:
+
+                        @pl.when(passes(way))
+                        def _():
+                            z_copy(i, owns[i], me, way, k + 1).wait_send()
+
+                    x_copy(i, owns[i], me, way * m + k).wait_send()
+                    core_copy(i, owns[i], me, way * m + k).wait()
+                    core_copy(i, owns[i], me, (2 + way) * m + k).wait()
+
+    begin(0)
     f1[me] = w1[...]
     f2[me] = w2[...]
     rec[me] = pk[me]
     rts[mine] = rt[...]
     gns[mine] = gn[...]
-
-    def z_step(i, k):
-        z[i][k].wait_recv()
-        at = lax.rem(a - k + m, m) * 4 + b * 2 + c
-        to_x(i, full[i].at[at], at, k)
-        to_core(i, full[i].at[at], at, k)
-
-    def x_step(i, k):
-        x[i][k].wait_recv()
-        at = lax.rem(a - k + m, m) * 4 + (1 - b) * 2 + c
-        to_core(i, full[i].at[at], at, m + k)
-
     for k in range(1, m):
-        z_step(0, k)
-    x_step(0, 0)
+        for way in range(2):
+            z_step(0, k, way)
+        if k == 1:
+            begin(1)
+            x_step(0, 0, 0)
+        else:
+            for way in range(2):
+                x_step(0, k - 1, way)
     for k in range(1, m):
-        z_step(1, k)
-        x_step(0, k)
-    for k in range(m):
-        x_step(1, k)
+        for way in range(2):
+            z_step(1, k, way)
+        if k == 1:
+            for way in range(2):
+                x_step(0, m - 1, way)
+    x_step(1, 0, 0)
+    for k in range(1, m):
+        for way in range(2):
+            x_step(1, k, way)
     for copy in small:
         copy.wait()
     for i in range(2):
-        for copy in z[i].values():
-            copy.wait_send()
-        for copy in x[i].values():
-            copy.wait_send()
-        for copy in core[i].values():
-            copy.wait()
+        finish(i)
 
 
 def spread(w1, w2, packed, right, gain, cid):
@@ -418,9 +438,9 @@
         in_specs=[VMEM] * 5,
         out_specs=(VMEM,) * 5,
         scratch_shapes=[
-            DMA((2, 2, m)),
-            DMA((2, 2, m)),
             DMA((2, 2, 2 * m)),
+            DMA((2, 2, 2 * m)),
+            DMA((2, 2, 4 * m)),
             DMA((2, n)),
             DMA((2, q)),
             DMA((2, q)),
@@ -521,7 +541,19 @@
     dhidden = jnp.sum(partial.astype(F32), 0)
     dact = dhidden * valid_col * act_sig * (1.0 + act * (1.0 - act_sig))
     row2 = jnp.concatenate([jnp.sum(dact, 0), jnp.sum(dact * normed_conv, 0)])[None]
-    row2, hidden_full = stats_hidden(row2, hidden, 2)
+    row2 = stats_sum(row2, 2)
+    mine = lax.axis_index("mp")
+    held = [hidden] + [
+        lax.ppermute(hidden, "mp", [(i, (i + k) % parts) for i in range(parts)])
+        for k in range(1, parts)
+    ]
+    placed = []
+    for p in range(parts):
+        block = held[0]
+        for k in range(1, parts):
+            block = jnp.where(lax.rem(mine - p + parts, parts) == k, held[k], block)
+        placed.append(block)
+    hidden_full = jnp.concatenate(placed, 1)
     grad_bias, grad_gain = row2[0, :half], row2[0, half:]
     encoded = (inputs + jnp.dot(hidden_full, weights_two, preferred_element_type=F32)).astype(
         BF16

time: 242 us -> 238 us (0.983)
  Pallas kernels: 164 us -> 144 us
  other arithmetic: 28.2 us -> 38 us
  local copies, waits for them, and re-layouts: 18.1 us -> 25.9 us
    pallas_call x1 -> x0, Pallas kernels: 17.6 us -> none  [stats_hidden(): pl.pallas_call(stats_hidden_kernel, out_shape=(jax.ShapeDtypeStruct(row.s...]
    reduce_sum x2, other arithmetic: 4.33 us -> 15.3 us  [kernel_terms(): jnp.sum(grad_shaped * padded[:, step:step + frames], axis=(0, 1))]
    another operation x32, local copies, waits for them, and re-layouts: 0.32 us -> 9.78 us  [kernel_terms(): return jnp.stack(rows_out, 0)]
    pallas_call x1, Pallas kernels: 64.4 us -> 56.6 us  [spread(): pl.pallas_call(functools.partial(spread_kernel, n), out_shape=(jax.ShapeD...]
    pallas_call x1 -> x2, Pallas kernels: 14.5 us -> 18.7 us  [stats_sum(): pl.pallas_call(stats_kernel, out_shape=jax.ShapeDtypeStruct(row.shape, F3...]
    unnamed x179 -> x67, local copies, waits for them, and re-layouts: 5.23 us -> 5.92 us
  transfers between devices with their start and end apart: 1 -> 2, of which waited for: 0 -> 0; matrix products, arithmetic and copies ran while one was open for 10% -> 17% of each run, Pallas kernels for 6% -> 5%
where the time goes in v3:
time: 238 us; the launch traced here: 237 us
  Pallas kernels  144 us (61%)
  other arithmetic  38 us (16%)
  local copies, waits for them, and re-layouts  25.9 us (11%)
  matrix products  21.9 us (9%)
  starting transfers between devices  6.38 us (3%)
    pallas_call x1, Pallas kernels, grads_sum(): pl.pallas_call(functools.partial(grads_kernel, n), out_shape=(jax.ShapeDt...  68.3 us
    pallas_call x1, Pallas kernels, spread(): pl.pallas_call(functools.partial(spread_kernel, n), out_shape=(jax.ShapeD...  56.6 us
    pallas_call x2, Pallas kernels, stats_sum(): pl.pallas_call(stats_kernel, out_shape=jax.ShapeDtypeStruct(row.shape, F3...  18.7 us
    reduce_sum x2, other arithmetic, kernel_terms(): jnp.sum(grad_shaped * padded[:, step:step + frames], axis=(0, 1))  15.3 us
    another operation x32, local copies, waits for them, and re-layouts, kernel_terms(): return jnp.stack(rows_out, 0)  9.78 us
    dot_general x2, matrix products, contract_rows(): lax.dot_general(left, right, (((0,), (0,)), ((), ())), preferred_element_...  7.63 us
    unnamed x67, local copies, waits for them, and re-layouts  5.92 us
  transfers between devices with their start and end apart: 2, of which 0 were waited for; matrix products, arithmetic and copies ran while one was open for 17% of the time, Pallas kernels for 5%

profile of v3, /device:TPU:8, one launch (start us, length us, event | category | flops | bytes accessed | tf_op | source)
XLA Modules:
  0.0 237.0 jit_solution(15306197251675538030)
XLA Ops:
  0.7 1.2 constant_dynamic-update-slice_fusion.1
  1.9 1.8 copy.29
  3.6 0.9 select_reduce_fusion.1
  4.6 1.3 fusion.80
  6.0 0.6 broadcast_in_dim.63.gn
  6.7 0.8 maximum_maximum_fusion.pk
  7.5 56.6 %spread.1 = (bf16[16,96,1536]{2,1,0:T(8,128)(2,1)}, bf16[16,96,768]{2,1,0:T(8,128)(2,1)}, bf16[16,16,384]{2,1,0:T(8,128)(2,1)}, bf16[2,448,768]{2,1,0:T(8,128)(2,1)}, f32[2,1,768]{2,1,0:T(1,128)}) custom-call(bf16[96,1536]{1,0:T(8,128)(2,1)} %bitcast.69, bf16[96,768]{1,0:T(8,128)(2,1)} %w2.1, bf16[16,16,384]{2,1,0:T(8,128)(2,1)} %maximum_maximum_fusion.pk, ...), custom_call_target="tpu_custom_call" | custom-call | tf_op jit(solution)/shard_map/spread/pallas_call | solution.py:429
  64.1 2.5 %fusion = bf16[256,1536]{0,1:T(8,128)(2,1)S(1)} fusion(bf16[1536,768]{1,0:T(8,128)(2,1)} %bitcast.80, bf16[256,768]{1,0:T(8,128)(2,1)S(1)} %copy-done.9), kind=kOutput, calls=%fused_computation.63 | convolution fusion | flops 604372992 | bytes 3538944 | tf_op jit(solution)/shard_map/dot_general | solution.py:536
  66.6 1.0 pad_maximum_fusion.2
  67.6 4.5 %all-to-all-start = ((bf16[2,256,768]{1,2,0:T(8,128)(2,1)}), bf16[2,256,768]{1,2,0:T(8,128)(2,1)}, u32[]{:S(2)}, u32[]{:S(2)}) async-start(bf16[2,256,768]{1,2,0:T(8,128)(2,1)} %pad_maximum_fusion.2), calls=%async_computation | async-start | bytes 1572864 | tf_op jit(solution)/shard_map/all_to_all | solution.py:540
  72.2 0.7 convert_reduce_fusion.2
  73.2 0.1 bitcast_multiply_fusion.1
  73.3 1.6 fusion.96
  74.9 1.9 fusion.95
  76.9 0.2 slice_reduce_fusion.31
  77.1 0.2 multiply_reduce_fusion
  77.3 0.3 copy-done.8
  77.6 4.3 %fusion.92 = f32[256,1536]{1,0:T(8,128)S(1)} fusion(bf16[1536,1536]{1,0:T(8,128)(2,1)} %bitcast.79, f32[256,768]{1,0:T(8,128)} %copy-done.7, f32[256,768]{1,0:T(8,128)} %copy-done.8, f32[1536]{0:T(1024)S(1)} %mul.793, f32[256]{0:T(256)S(1)} %get-tuple-element.100, f32[256]{0:T(256)S(1)} %get-tuple-element.101), kind=kOutput, calls=%fused_computation.267 | convolution fusion | flops 1209925632 | bytes 7872512 | tf_op jit(solution)/shard_map/dot_general | solution.py:514
  81.9 0.2 multiply_multiply_fusion.1
  82.2 0.9 copy-done.2
  83.0 3.4 %multiply_reduce_fusion.1 = (f32[768]{0:T(1024)S(1)}, f32[768]{0:T(1024)S(1)}, f32[16,16,768]{2,1,0:T(8,128)}) fusion(f32[16,16]{1,0:T(8,128)S(1)} %fusion.82, f32[768]{0:T(1024)S(1)} %get-tuple-element.88, f32[768]{0:T(1024)S(1)} %get-tuple-element.89, f32[768]{0:T(1024)S(1)} %get-tuple-element.60, f32[768]{0:T(1024)S(1)} %get-tuple-element.61, ...), kind=kLoop, calls=%fused_computation.71 | loop fusion | flops 12777984 | bytes 1675264 | tf_op jit(solution)/shard_map/reduce_sum | solution.py:522
  86.5 0.7 fusion.85
  87.1 0.6 broadcast_in_dim.65
  87.8 0.6 broadcast_in_dim.66.x_ref
  88.4 10.7 %stats_sum.2 = f32[1,1664]{1,0:T(1,128)} custom-call(f32[1,1664]{1,0:T(1,128)} %broadcast_in_dim.66.x_ref), custom_call_target="tpu_custom_call" | custom-call | tf_op jit(solution)/shard_map/stats_sum/pallas_call | solution.py:116
  99.1 1.2 slice.454
  100.3 1.4 fusion.94
  101.7 2.2 convert_reduce_fusion
  103.9 2.3 copy.28
  106.2 2.7 %fusion.93 = (f32[768]{0:T(1024)S(1)}, f32[768]{0:T(1024)S(1)}, f32[16,16,768]{2,1,0:T(8,128)}) fusion(f32[768]{0:T(1024)S(1)} %get-tuple-element.94, f32[16,16,768]{2,1,0:T(8,128)} %get-tuple-element.99, f32[768]{0:T(1024)S(1)} %get-tuple-element.93, f32[768]{0:T(1024)S(1)} %copy-done.15, f32[768]{0:T(1024)S(1)} %copy-done.14, f32[16,16]{1,0:T(8,128)S(1)} %fusion.82, ...), kind=kLoop, calls=%fused_computation.268 | loop fusion | flops 3144192 | bytes 2378752 | tf_op jit(solution)/shard_map/reduce_sum | solution.py:543
  108.9 0.6 broadcast_in_dim.67.x_ref
  109.5 8.0 %stats_sum.3 = f32[1,1536]{1,0:T(1,128)} custom-call(f32[1,1536]{1,0:T(1,128)} %broadcast_in_dim.67.x_ref), custom_call_target="tpu_custom_call" | custom-call | tf_op jit(solution)/shard_map/stats_sum/pallas_call | solution.py:116
  117.5 2.0 slice_reduce_fusion.32
  119.5 9.2 %multiply_reduce_fusion.2 = (f32[768]{0:T(1024)}, f32[768]{0:T(1024)}, f32[768]{0:T(1024)}, f32[768]{0:T(1024)}, f32[768]{0:T(1024)}, /*index=5*/f32[768]{0:T(10...) fusion(f32[16,16,768]{2,1,0:T(8,128)} %bitcast.65, ...), kind=kLoop, calls=%fused_computation.147 | loop fusion | flops 8833536 | bytes 3217412 | tf_op jit(solution)/shard_map/reduce_sum | solution.py:44
  128.7 2.4 %fusion.54 = f32[16,16,768]{2,1,0:T(8,128)S(1)} fusion(f32[16,16,768]{2,1,0:T(8,128)S(1)} %get-tuple-element.97, f32[768]{0:T(1024)S(1)} %get-tuple-element.88, f32[768]{0:T(1024)S(1)} %get-tuple-element.89, f32[768]{0:T(1024)S(1)} %get-tuple-element.60, f32[768]{0:T(1024)S(1)} %get-tuple-element.61, f32[768]{0:T(1024)S(1)} %get-tuple-element.62, ...), kind=kLoop, calls=%fused_computation.124 | loop fusion | flops 11993088 | bytes 1668096 | tf_op jit(solution)/shard_map/add | solution.py:32
  131.1 1.5 multiply_convert_fusion.2
  132.7 1.9 collective-permute-start
  134.5 1.3 fusion.78
  135.8 6.1 %multiply_reduce_fusion.21 = (f32[768]{0:T(1024)S(1)}, f32[768]{0:T(1024)S(1)}, f32[768]{0:T(1024)S(1)}, f32[768]{0:T(1024)S(1)}, f32[768]{0:T(1024)S(1)}, /*ind...) fusion(f32[16,16,768]{2,1,0:T(8,128)} %copy-done.3, ...), kind=kLoop, calls=%fused_computation.166 | loop fusion | flops 6084864 | bytes 3186688 | tf_op jit(solution)/shard_map/reduce_sum | solution.py:44
  142.1 0.7 stack.132
  142.7 0.7 stack.133
  143.4 0.7 stack.134
  144.1 0.7 stack.136
  144.8 0.7 stack.137
  145.5 0.7 stack.138
  146.1 0.7 stack.139
  146.8 0.7 stack.140
  147.5 0.7 stack.141
  148.2 0.7 stack.142
  148.9 0.7 stack.143
  149.6 0.7 stack.144
  150.2 0.7 stack.145
  150.9 0.7 stack.146
  151.7 0.2 stack.151
  151.9 0.6 pad.14
  152.5 5.3 %convolution_convert_fusion = bf16[1536,1536]{1,0:T(8,128)(2,1)} fusion(bf16[256,768]{1,0:T(8,128)(2,1)} %get-tuple-element.103, bf16[256,768]{1,0:T(8,128)(2,1)} %get-tuple-element.102, f32[256,768]{1,0:T(8,128)} %copy-done.7, f32[256,768]{1,0:T(8,128)} %copy-done.8, f32[1536]{0:T(1024)S(1)} %copy-done.24, f32[256]{0:T(256)S(1)} %copy-done.28, ...), kind=kOutput, calls=%fused_computation.60 | convolution fusion | flops 1213857792 | bytes 7086080 | tf_op jit(solution)/shard_map/dot_general | solution.py:49
  157.9 1.2 broadcast_select_fusion.1
  159.1 2.3 convolution_convert_fusion.1
  161.4 1.5 fusion.1
  162.9 68.3 %grads_sum.1 = (f32[96,1536]{1,0:T(8,128)}, f32[96,768]{1,0:T(8,128)}, f32[16,1,1536]{2,1,0:T(1,128)}) custom-call(bf16[4,2,2,96,1536]{4,3,2,1,0:T(8,128)(2,1)} %bitcast.68, bf16[4,2,2,96,768]{4,3,2,1,0:T(8,128)(2,1)} %bitcast.67, f32[16,1,1536]{2,1,0:T(1,128)} %bitcast.70), custom_call_target="tpu_custom_call" | custom-call | tf_op jit(solution)/shard_map/grads_sum/pallas_call | solution.py:248
  231.2 2.3 reshape.294
  233.5 1.1 reduce.45
  234.6 0.7 slice.490
  235.3 1.7 copy.34
  (102 shorter events, 1.0 us)
Async XLA Ops:
  0.6 4.0 %copy-start = (bf16[128,16,320]{0,2,1:T(8,128)(2,1)S(1)}, bf16[128,16,320]{0,2,1:T(8,128)(2,1)}, u32[]{:S(2)}) copy-start(bf16[128,16,320]{0,2,1:T(8,128)(2,1)} %param.13) | copy-start | bytes 3932164
  0.6 5.3 %copy-start.26 = (f32[768]{0:T(1024)S(1)}, f32[768]{0:T(1024)}, u32[]{:S(2)}) copy-start(f32[768]{0:T(1024)} %param.19) | copy-start | bytes 9220
  0.7 5.9 %copy-start.12 = (bf16[128,768]{1,0:T(8,128)(2,1)S(1)}, bf16[128,768]{1,0:T(8,128)(2,1)}, u32[]{:S(2)}) copy-start(bf16[128,768]{1,0:T(8,128)(2,1)} %param.18) | copy-start | bytes 589828
  1.8 62.2 %copy-start.9 = (bf16[256,768]{1,0:T(8,128)(2,1)S(1)}, bf16[256,768]{1,0:T(8,128)(2,1)}, u32[]{:S(2)}) copy-start(bf16[256,768]{1,0:T(8,128)(2,1)} %param.25) | copy-start | bytes 1179652
  6.6 0.9 copy-start.4
  66.6 5.6 %copy-start.11 = (bf16[16,16,384]{2,1,0:T(8,128)(2,1)S(1)}, bf16[16,16,384]{2,1,0:T(8,128)(2,1)}, u32[]{:S(2)}) copy-start(bf16[16,16,384]{2,1,0:T(8,128)(2,1)} %get-tuple-element.14) | copy-start | bytes 589828
  67.6 34.1 %all-to-all-start = ((bf16[2,256,768]{1,2,0:T(8,128)(2,1)}), bf16[2,256,768]{1,2,0:T(8,128)(2,1)}, u32[]{:S(2)}, u32[]{:S(2)}) async-start(bf16[2,256,768]{1,2,0:T(8,128)(2,1)} %pad_maximum_fusion.2), calls=%async_computation | async-start | bytes 1572864 | tf_op jit(solution)/shard_map/all_to_all | solution.py:540
  72.1 4.6 %copy-start.13 = (f32[31,768]{1,0:T(8,128)S(1)}, f32[31,768]{1,0:T(8,128)}, u32[]{:S(2)}) copy-start(f32[31,768]{1,0:T(8,128)} %param.21) | copy-start | bytes 285700
  72.1 4.9 %copy-start.25 = (f32[2,1,768]{2,1,0:T(1,128)S(1)}, f32[2,1,768]{2,1,0:T(1,128)}, u32[]{:S(2)}) copy-start(f32[2,1,768]{2,1,0:T(1,128)} %get-tuple-element.16) | copy-start | bytes 18436
  73.1 8.7 %copy-start.16 = (f32[256]{0:T(256)}, f32[256]{0:T(256)S(1)}, u32[]{:S(2)}) copy-start(f32[256]{0:T(256)S(1)} %reshape.296) | copy-start | bytes 3076
  74.9 2.5 %copy-start.7 = (f32[256,768]{1,0:T(8,128)}, f32[256,768]{1,0:T(8,128)S(1)}, u32[]{:S(2)}) copy-start(f32[256,768]{1,0:T(8,128)S(1)} %get-tuple-element.112) | copy-start | bytes 2359300
  76.7 0.9 copy-start.8
  77.1 4.8 %copy-start.23 = (f32[1536]{0:T(1024)}, f32[1536]{0:T(1024)S(1)}, u32[]{:S(2)}) copy-start(f32[1536]{0:T(1024)S(1)} %mul.793) | copy-start | bytes 18436
  77.3 4.6 %copy-start.27 = (f32[256]{0:T(256)}, f32[256]{0:T(256)S(1)}, u32[]{:S(2)}) copy-start(f32[256]{0:T(256)S(1)} %get-tuple-element.100) | copy-start | bytes 3076
  77.3 4.6 %copy-start.29 = (f32[256]{0:T(256)}, f32[256]{0:T(256)S(1)}, u32[]{:S(2)}) copy-start(f32[256]{0:T(256)S(1)} %get-tuple-element.101) | copy-start | bytes 3076
  82.2 0.9 copy-start.2
  83.0 23.2 %copy-start.14 = (f32[768]{0:T(1024)S(1)}, f32[768]{0:T(1024)}, u32[]{:S(2)}) copy-start(f32[768]{0:T(1024)} %param.22) | copy-start | bytes 9220
  83.0 23.2 %copy-start.15 = (f32[768]{0:T(1024)S(1)}, f32[768]{0:T(1024)}, u32[]{:S(2)}) copy-start(f32[768]{0:T(1024)} %param.23) | copy-start | bytes 9220
  119.5 9.2 %copy-start.18 = (f32[768]{0:T(1024)}, f32[768]{0:T(1024)S(1)}, u32[]{:S(2)}) copy-start(f32[768]{0:T(1024)S(1)} %get-tuple-element.125) | copy-start | bytes 9220
  119.5 11.6 %copy-start.1 = (f32[16,16,768]{2,1,0:T(8,128)S(1)}, f32[16,16,768]{2,1,0:T(8,128)}, u32[]{:S(2)}) copy-start(f32[16,16,768]{2,1,0:T(8,128)} %get-tuple-element.99) | copy-start | bytes 2359300
  119.5 11.6 %copy-start.17 = (f32[256]{0:T(256)S(1)}, f32[256]{0:T(256)}, u32[]{:S(2)}) copy-start(f32[256]{0:T(256)} %copy-done.16) | copy-start | bytes 3076
  128.7 4.0 %copy-start.3 = (f32[16,16,768]{2,1,0:T(8,128)}, f32[16,16,768]{2,1,0:T(8,128)S(1)}, u32[]{:S(2)}) copy-start(f32[16,16,768]{2,1,0:T(8,128)S(1)} %get-tuple-element.97) | copy-start | bytes 2359300
  131.1 3.4 %copy-start.5 = (bf16[448,768]{1,0:T(8,128)(2,1)S(1)}, bf16[448,768]{1,0:T(8,128)(2,1)}, u32[]{:S(2)}) copy-start(bf16[448,768]{1,0:T(8,128)(2,1)} %copy-done.4) | copy-start | bytes 2064388
  132.7 18.9 %copy-start.22 = (f32[768]{0:T(1024)S(1)}, f32[768]{0:T(1024)}, u32[]{:S(2)}) copy-start(f32[768]{0:T(1024)} %get-tuple-element.25) | copy-start | bytes 9220
  132.7 18.9 %copy-start.21 = (f32[768]{0:T(1024)S(1)}, f32[768]{0:T(1024)}, u32[]{:S(2)}) copy-start(f32[768]{0:T(1024)} %get-tuple-element.24) | copy-start | bytes 9220
  132.7 18.9 %copy-start.20 = (f32[768]{0:T(1024)S(1)}, f32[768]{0:T(1024)}, u32[]{:S(2)}) copy-start(f32[768]{0:T(1024)} %get-tuple-element.23) | copy-start | bytes 9220
  132.7 19.0 %copy-start.19 = (f32[768]{0:T(1024)S(1)}, f32[768]{0:T(1024)}, u32[]{:S(2)}) copy-start(f32[768]{0:T(1024)} %get-tuple-element.22) | copy-start | bytes 9220
  132.7 25.2 %collective-permute-start = (bf16[256,768]{1,0:T(8,128)(2,1)S(1)}, bf16[256,768]{1,0:T(8,128)(2,1)}, u32[]{:S(2)}, u32[]{:S(2)}) collective-permute-start(bf16[256,768]{1,0:T(8,128)(2,1)S(1)} %get-tuple-element.108), channel_id=1, source_target_pairs={{0,1},{1,0},{2,3},{3,2},{4,5},{5,4},{6,7},{7,6},{8,9},{9,8},{10,11... | collective-permute-start | bytes 1179656 | tf_op jit(solution)/shard_map/ppermute | solution.py:547
  135.8 16.7 %copy-start.24 = (f32[1536]{0:T(1024)S(1)}, f32[1536]{0:T(1024)}, u32[]{:S(2)}) copy-start(f32[1536]{0:T(1024)} %copy-done.23) | copy-start | bytes 18436
  135.8 16.7 %copy-start.28 = (f32[256]{0:T(256)S(1)}, f32[256]{0:T(256)}, u32[]{:S(2)}) copy-start(f32[256]{0:T(256)} %copy-done.27) | copy-start | bytes 3076
  135.8 16.7 %copy-start.30 = (f32[256]{0:T(256)S(1)}, f32[256]{0:T(256)}, u32[]{:S(2)}) copy-start(f32[256]{0:T(256)} %copy-done.29) | copy-start | bytes 3076
  152.5 6.6 %copy-start.10 = (bf16[256,768]{1,0:T(8,128)(2,1)S(1)}, bf16[256,768]{1,0:T(8,128)(2,1)}, u32[]{:S(2)}) copy-start(bf16[256,768]{1,0:T(8,128)(2,1)} %param.25) | copy-start | bytes 1179652
  157.9 3.5 %copy-start.6 = (f32[256,768]{1,0:T(8,128)S(1)}, f32[256,768]{1,0:T(8,128)}, u32[]{:S(2)}) copy-start(f32[256,768]{1,0:T(8,128)} %fusion.78) | copy-start | bytes 2359300
  157.9 3.5 %copy-start.31 = (bf16[16,96,768]{2,1,0:T(8,128)(2,1)S(1)}, bf16[16,96,768]{2,1,0:T(8,128)(2,1)}, u32[]{:S(2)}) copy-start(bf16[16,96,768]{2,1,0:T(8,128)(2,1)} %get-tuple-element.18) | copy-start | bytes 7077892

commit v4 on v3

--- a/solution.py
+++ b/solution.py
@@ -122,6 +122,52 @@
         compiler_params=pltpu.CompilerParams(collective_id=cid, has_side_effects=True),
         name="stats_sum",
     )(row)
+
+
+def stats_hidden_kernel(
+    x_ref, h_ref, o_ref, hid_ref, slots, hslots, send, recv, hsend, hrecv
+):
+    size, me = lax.axis_size("dp"), lax.axis_index("dp")
+    parts, mine = lax.axis_size("mp"), lax.axis_index("mp")
+    chans = h_ref.shape[1]
+    greet(("dp", "mp"))
+    copies = push_all("dp", lambda peer: x_ref, slots, send, recv)
+    wide = push_all("mp", lambda peer: h_ref, hslots, hsend, hrecv)
+    slots[me] = x_ref[...]
+    hslots[mine] = h_ref[...]
+    for copy in copies:
+        copy.wait()
+    o_ref[...] = sum_slots(slots, size)
+    for copy in wide:
+        copy.wait()
+    for p in range(parts):
+        hid_ref[:, p * chans : (p + 1) * chans] = hslots[p]
+
+
+def stats_hidden(row, hidden, cid):
+    n, q = lax.axis_size("dp"), lax.axis_size("mp")
+    rows, chans = hidden.shape
+    return pl.pallas_call(
+        stats_hidden_kernel,
+        out_shape=(
+            jax.ShapeDtypeStruct(row.shape, F32),
+            jax.ShapeDtypeStruct((rows, q * chans), BF16),
+        ),
+        in_specs=[VMEM, VMEM],
+        out_specs=(VMEM, VMEM),
+        scratch_shapes=[
+            pltpu.VMEM((n,) + row.shape, F32),
+            pltpu.VMEM((q,) + hidden.shape, BF16),
+            DMA((n,)),
+            DMA((n,)),
+            DMA((q,)),
+            DMA((q,)),
+        ],
+        compiler_params=pltpu.CompilerParams(
+            collective_id=cid, has_side_effects=True, vmem_limit_bytes=LIMIT
+        ),
+        name="stats_hidden",
+    )(row, hidden)
 
 
 def grads_kernel(
@@ -541,19 +587,7 @@
     dhidden = jnp.sum(partial.astype(F32), 0)
     dact = dhidden * valid_col * act_sig * (1.0 + act * (1.0 - act_sig))
     row2 = jnp.concatenate([jnp.sum(dact, 0), jnp.sum(dact * normed_conv, 0)])[None]
-    row2 = stats_sum(row2, 2)
-    mine = lax.axis_index("mp")
-    held = [hidden] + [
-        lax.ppermute(hidden, "mp", [(i, (i + k) % parts) for i in range(parts)])
-        for k in range(1, parts)
-    ]
-    placed = []
-    for p in range(parts):
-        block = held[0]
-        for k in range(1, parts):
-            block = jnp.where(lax.rem(mine - p + parts, parts) == k, held[k], block)
-        placed.append(block)
-    hidden_full = jnp.concatenate(placed, 1)
+    row2, hidden_full = stats_hidden(row2, hidden, 2)
     grad_bias, grad_gain = row2[0, :half], row2[0, half:]
     encoded = (inputs + jnp.dot(hidden_full, weights_two, preferred_element_type=F32)).astype(
         BF16

time: 238 us -> 229 us (0.962)
  other arithmetic: 38 us -> 28.2 us
  Pallas kernels: 144 us -> 152 us
  local copies, waits for them, and re-layouts: 25.9 us -> 18.1 us
    pallas_call x0 -> x1, Pallas kernels: none -> 15.6 us  [stats_hidden(): pl.pallas_call(stats_hidden_kernel, out_shape=(jax.ShapeDtypeStruct(row.s...]
    reduce_sum x2, other arithmetic: 15.3 us -> 4.33 us  [kernel_terms(): jnp.sum(grad_shaped * padded[:, step:step + frames], axis=(0, 1))]
    another operation x32, local copies, waits for them, and re-layouts: 9.78 us -> 0.32 us  [kernel_terms(): return jnp.stack(rows_out, 0)]
    pallas_call x2 -> x1, Pallas kernels: 18.7 us -> 10.7 us  [stats_sum(): pl.pallas_call(stats_kernel, out_shape=jax.ShapeDtypeStruct(row.shape, F3...]
    unnamed x67 -> x179, local copies, waits for them, and re-layouts: 5.92 us -> 5.23 us
  transfers between devices with their start and end apart: 2 -> 1, of which waited for: 0 -> 0; matrix products, arithmetic and copies ran while one was open for 17% -> 11% of each run, Pallas kernels for 5% -> 5%
where the time goes in v4:
time: 229 us; the launch traced here: 228 us
  Pallas kernels  152 us (66%)
  other arithmetic  28.2 us (12%)
  matrix products  24 us (10%)
  local copies, waits for them, and re-layouts  18.1 us (8%)
  starting transfers between devices  4.34 us (2%)
    pallas_call x1, Pallas kernels, grads_sum(): pl.pallas_call(functools.partial(grads_kernel, n), out_shape=(jax.ShapeDt...  68.6 us
    pallas_call x1, Pallas kernels, spread(): pl.pallas_call(functools.partial(spread_kernel, n), out_shape=(jax.ShapeD...  56.6 us
    pallas_call x1, Pallas kernels, stats_hidden(): pl.pallas_call(stats_hidden_kernel, out_shape=(jax.ShapeDtypeStruct(row.s...  15.6 us
    pallas_call x1, Pallas kernels, stats_sum(): pl.pallas_call(stats_kernel, out_shape=jax.ShapeDtypeStruct(row.shape, F3...  10.7 us
    dot_general x2, matrix products, contract_rows(): lax.dot_general(left, right, (((0,), (0,)), ((), ())), preferred_element_...  7.46 us
    unnamed x179, local copies, waits for them, and re-layouts  5.23 us
  transfers between devices with their start and end apart: 1, of which 0 were waited for; matrix products, arithmetic and copies ran while one was open for 11% of the time, Pallas kernels for 5%

profile of v4, /device:TPU:8, one launch (start us, length us, event | category | flops | bytes accessed | tf_op | source)
XLA Modules:
  0.0 228.4 jit_solution(10294239090527401962)
XLA Ops:
  0.6 0.0 copy-start
  0.7 1.8 copy.29
  2.5 0.9 select_reduce_fusion.1
  3.4 0.1 copy.27
  3.5 1.3 fusion.79
  5.0 0.6 broadcast_in_dim.63.gn
  5.6 0.1 pad.30.clone
  5.7 0.9 maximum_maximum_fusion.pk
  6.6 56.6 %spread.1 = (bf16[16,96,1536]{2,1,0:T(8,128)(2,1)}, bf16[16,96,768]{2,1,0:T(8,128)(2,1)}, bf16[16,16,384]{2,1,0:T(8,128)(2,1)}, bf16[2,448,768]{2,1,0:T(8,128)(2,1)}, f32[2,1,768]{2,1,0:T(1,128)}) custom-call(bf16[96,1536]{1,0:T(8,128)(2,1)} %bitcast.71, bf16[96,768]{1,0:T(8,128)(2,1)} %w2.1, bf16[16,16,384]{2,1,0:T(8,128)(2,1)} %maximum_maximum_fusion.pk, ...), custom_call_target="tpu_custom_call" | custom-call | tf_op jit(solution)/shard_map/spread/pallas_call | solution.py:475
  63.2 2.5 %fusion = bf16[256,1536]{0,1:T(8,128)(2,1)S(1)} fusion(bf16[1536,768]{1,0:T(8,128)(2,1)} %bitcast.82, bf16[256,768]{1,0:T(8,128)(2,1)S(1)} %copy-done.10), kind=kOutput, calls=%fused_computation.63 | convolution fusion | flops 604372992 | bytes 3538944 | tf_op jit(solution)/shard_map/dot_general | solution.py:582
  65.7 0.0 copy-start.13
  65.7 0.1 slice_bitcast_fusion.1
  65.7 1.0 pad_maximum_fusion.1
  66.7 4.3 %all-to-all-start = ((bf16[2,256,768]{1,2,0:T(8,128)(2,1)}), bf16[2,256,768]{1,2,0:T(8,128)(2,1)}, u32[]{:S(2)}, u32[]{:S(2)}) async-start(bf16[2,256,768]{1,2,0:T(8,128)(2,1)} %pad_maximum_fusion.1), calls=%async_computation | async-start | bytes 1572864 | tf_op jit(solution)/shard_map/all_to_all | solution.py:586
  71.1 0.7 convert_reduce_fusion.2
  71.8 0.7 fusion.84
  72.5 0.1 fusion.81
  72.6 0.7 slice_reduce_fusion.30
  73.3 0.7 slice_reduce_fusion.31
  74.0 0.1 fusion.82
  74.1 0.1 reshape.298
  74.2 0.1 bitcast_multiply_fusion.1
  74.3 0.4 copy-done.77
  74.7 2.1 fusion.93
  76.9 2.4 %fusion.92 = (f32[256]{0:T(256)}, f32[256,768]{1,0:T(8,128)S(1)}) fusion(bf16[2,448,768]{2,1,0:T(8,128)(2,1)} %get-tuple-element.18, bf16[256,128]{1,0:T(8,128)(2,1)S(1)} %bitcast.75, bf16[256,320]{1,0:T(8,128)(2,1)S(1)} %bitcast_multiply_fusion.1), kind=kOutput, calls=%fused_computation.264 | convolution fusion | flops 176815872 | bytes 1704960 | tf_op jit(solution)/shard_map/dot_general | solution.py:552
  79.3 1.3 reduce.10
  80.6 1.3 mul.794
  81.9 0.2 multiply_reduce_fusion
  82.1 0.7 add_rsqrt_fusion
  82.8 4.3 %fusion.89 = f32[256,1536]{1,0:T(8,128)S(1)} fusion(bf16[1536,1536]{1,0:T(8,128)(2,1)} %bitcast.81, f32[256,768]{1,0:T(8,128)} %copy-done.7, f32[256,768]{1,0:T(8,128)} %copy-done.8, f32[1536]{0:T(1024)} %mul.794, f32[256]{0:T(256)S(1)} %get-tuple-element.104, f32[256]{0:T(256)S(1)} %get-tuple-element.105), kind=kOutput, calls=%fused_computation.261 | convolution fusion | flops 1209925632 | bytes 7872512 | tf_op jit(solution)/shard_map/dot_general | solution.py:560
  87.3 0.0 copy-start.53
  87.4 0.2 multiply_multiply_fusion.1
  87.7 0.9 copy-done.1
  88.8 3.6 %multiply_reduce_fusion.1 = (f32[768]{0:T(1024)S(1)}, f32[768]{0:T(1024)S(1)}, f32[16,16,768]{2,1,0:T(8,128)}) fusion(f32[16,16]{1,0:T(8,128)S(1)} %fusion.81, f32[768]{0:T(1024)S(1)} %copy-done.73, f32[768]{0:T(1024)S(1)} %copy-done.75, f32[768]{0:T(1024)S(1)} %get-tuple-element.64, f32[768]{0:T(1024)S(1)} %copy-done.19, f32[768]{0:T(1024)S(1)} %copy-done.21, ...), kind=kLoop, calls=%fused_computation.71 | loop fusion | flops 12777984 | bytes 1675264 | tf_op jit(solution)/shard_map/reduce_sum | solution.py:568
  92.5 0.6 broadcast_in_dim.65
  93.1 0.6 broadcast_in_dim.66.x_ref
  93.7 10.7 %stats_sum.1 = f32[1,1664]{1,0:T(1,128)} custom-call(f32[1,1664]{1,0:T(1,128)} %broadcast_in_dim.66.x_ref), custom_call_target="tpu_custom_call" | custom-call | tf_op jit(solution)/shard_map/stats_sum/pallas_call | solution.py:116
  104.4 1.2 slice.456
  105.6 1.3 fusion.91
  106.9 2.2 multiply_convert_fusion.3.h_ref
  109.1 0.0 all-to-all-done
  109.1 2.2 convert_reduce_fusion
  111.3 2.3 %copy.28 = f32[256,768]{1,0:T(8,128)} copy(f32[256,768]{0,1:T(8,128)} %convert_reduce_fusion) | data formatting | bytes 1572864 | tf_op jit(solution)/shard_map/reduce_sum | solution.py:587
  113.6 1.9 fusion.90
  115.5 0.6 broadcast_in_dim.67.x_ref
  116.1 15.6 %stats_hidden.1 = (f32[1,1536]{1,0:T(1,128)}, bf16[256,1536]{1,0:T(8,128)(2,1)}) custom-call(f32[1,1536]{1,0:T(1,128)} %broadcast_in_dim.67.x_ref, bf16[256,768]{1,0:T(8,128)(2,1)} %multiply_convert_fusion.3.h_ref), custom_call_target="tpu_custom_call" | custom-call | tf_op jit(solution)/shard_map/stats_hidden/pallas_call | solution.py:150
  131.7 2.7 %fusion.94 = f32[256,768]{1,0:T(8,128)S(1)} fusion(bf16[256,1536]{1,0:T(8,128)(2,1)} %get-tuple-element.21, bf16[1536,768]{1,0:T(8,128)(2,1)} %bitcast.83), kind=kOutput, calls=%fused_computation.266 | convolution fusion | flops 603979776 | bytes 3932160 | tf_op jit(solution)/shard_map/dot_general | solution.py:592
  134.5 0.0 copy-start.14
  134.5 2.3 convolution_convert_fusion.1
  137.0 0.0 copy-start.54
  137.1 1.2 slice_reduce_fusion.32
  138.3 2.6 %multiply_reduce_fusion.2 = (f32[768]{0:T(1024)S(1)}, f32[768]{0:T(1024)S(1)}, f32[768]{0:T(1024)S(1)}, f32[768]{0:T(1024)S(1)}, f32[768]{0:T(1024)S(1)}, /*inde...) fusion(f32[16,16,768]{2,1,0:T(8,128)S(1)} %bitcast.67, ...), kind=kLoop, calls=%fused_computation.146 | loop fusion | flops 8833536 | bytes 3217412 | tf_op jit(solution)/shard_map/reduce_sum | solution.py:44
  141.2 2.5 %fusion.54 = f32[16,16,768]{2,1,0:T(8,128)S(1)} fusion(f32[16,16,768]{2,1,0:T(8,128)S(1)} %get-tuple-element.101, f32[768]{0:T(1024)S(1)} %copy-done.74, f32[768]{0:T(1024)S(1)} %copy-done.76, f32[768]{0:T(1024)S(1)} %copy-done.18, f32[768]{0:T(1024)S(1)} %copy-done.20, f32[768]{0:T(1024)S(1)} %copy-done.22, f32[768]{0:T(1024)S(1)} %copy-done.24, ...), kind=kLoop, calls=%fused_computation.124 | loop fusion | flops 11993088 | bytes 1668096 | tf_op jit(solution)/shard_map/add | solution.py:32
  143.7 1.7 multiply_reduce_fusion.21
  145.5 1.1 fusion.1
  146.6 1.1 multiply_convert_fusion.2
  148.0 0.2 stack.151
  148.3 5.2 %convolution_convert_fusion = bf16[1536,1536]{1,0:T(8,128)(2,1)} fusion(bf16[256,768]{1,0:T(8,128)(2,1)} %get-tuple-element.107, bf16[256,768]{1,0:T(8,128)(2,1)S(1)} %get-tuple-element.106, f32[256,768]{1,0:T(8,128)} %copy-done.7, f32[256,768]{1,0:T(8,128)} %copy-done.8, f32[1536]{0:T(1024)S(1)} %copy-done.81, f32[256]{0:T(256)S(1)} %copy-done.85, ...), kind=kOutput, calls=%fused_computation.60 | convolution fusion | flops 1213857792 | bytes 7086080 | tf_op jit(solution)/shard_map/dot_general | solution.py:49
  153.5 0.6 pad.14
  154.1 68.6 %grads_sum.1 = (f32[96,1536]{1,0:T(8,128)}, f32[96,768]{1,0:T(8,128)}, f32[16,1,1536]{2,1,0:T(1,128)}) custom-call(bf16[4,2,2,96,1536]{4,3,2,1,0:T(8,128)(2,1)} %bitcast.70, bf16[4,2,2,96,768]{4,3,2,1,0:T(8,128)(2,1)} %bitcast.69, f32[16,1,1536]{2,1,0:T(1,128)} %bitcast.72), custom_call_target="tpu_custom_call" | custom-call | tf_op jit(solution)/shard_map/grads_sum/pallas_call | solution.py:294
  222.7 2.3 reshape.296
  225.0 1.1 reduce.45
  226.1 0.7 slice.490
  226.8 1.7 copy.34
  (212 shorter events, 0.6 us)
Async XLA Ops:
  0.6 2.9 %copy-start = (bf16[128,16,320]{0,2,1:T(8,128)(2,1)S(1)}, bf16[128,16,320]{0,2,1:T(8,128)(2,1)}, u32[]{:S(2)}) copy-start(bf16[128,16,320]{0,2,1:T(8,128)(2,1)} %param.13) | copy-start | bytes 3932164
  0.6 4.3 %copy-start.9 = (bf16[320,768]{1,0:T(8,128)(2,1)S(1)}, bf16[320,768]{1,0:T(8,128)(2,1)}, u32[]{:S(2)}) copy-start(bf16[320,768]{1,0:T(8,128)(2,1)} %param.17) | copy-start | bytes 1474564
  0.7 4.3 %copy-start.83 = (f32[768]{0:T(1024)S(1)}, f32[768]{0:T(1024)}, u32[]{:S(2)}) copy-start(f32[768]{0:T(1024)} %param.19) | copy-start | bytes 9220
  0.7 5.0 %copy-start.12 = (bf16[128,768]{1,0:T(8,128)(2,1)S(1)}, bf16[128,768]{1,0:T(8,128)(2,1)}, u32[]{:S(2)}) copy-start(bf16[128,768]{1,0:T(8,128)(2,1)} %param.18) | copy-start | bytes 589828
  3.5 59.7 %copy-start.10 = (bf16[256,768]{1,0:T(8,128)(2,1)S(1)}, bf16[256,768]{1,0:T(8,128)(2,1)}, u32[]{:S(2)}) copy-start(bf16[256,768]{1,0:T(8,128)(2,1)} %param.25) | copy-start | bytes 1179652
  65.7 5.4 %copy-start.11 = (bf16[16,16,384]{2,1,0:T(8,128)(2,1)S(1)}, bf16[16,16,384]{2,1,0:T(8,128)(2,1)}, u32[]{:S(2)}) copy-start(bf16[16,16,384]{2,1,0:T(8,128)(2,1)} %get-tuple-element.16) | copy-start | bytes 589828
  65.7 6.9 %copy-start.13 = (f32[31,768]{1,0:T(8,128)S(1)}, f32[31,768]{1,0:T(8,128)}, u32[]{:S(2)}) copy-start(f32[31,768]{1,0:T(8,128)} %param.21) | copy-start | bytes 285700
  66.7 42.4 %all-to-all-start = ((bf16[2,256,768]{1,2,0:T(8,128)(2,1)}), bf16[2,256,768]{1,2,0:T(8,128)(2,1)}, u32[]{:S(2)}, u32[]{:S(2)}) async-start(bf16[2,256,768]{1,2,0:T(8,128)(2,1)} %pad_maximum_fusion.1), calls=%async_computation | async-start | bytes 1572864 | tf_op jit(solution)/shard_map/all_to_all | solution.py:586
  74.0 13.7 %copy-start.15 = (f32[768]{0:T(1024)}, f32[768]{0:T(1024)S(1)}, u32[]{:S(2)}) copy-start(f32[768]{0:T(1024)S(1)} %get-tuple-element.63) | copy-start | bytes 9220
  74.0 13.7 %copy-start.17 = (f32[768]{0:T(1024)}, f32[768]{0:T(1024)S(1)}, u32[]{:S(2)}) copy-start(f32[768]{0:T(1024)S(1)} %get-tuple-element.64) | copy-start | bytes 9220
  76.9 5.9 %copy-start.7 = (f32[256,768]{1,0:T(8,128)}, f32[256,768]{1,0:T(8,128)S(1)}, u32[]{:S(2)}) copy-start(f32[256,768]{1,0:T(8,128)S(1)} %get-tuple-element.113) | copy-start | bytes 2359300
  79.3 3.5 %copy-start.8 = (f32[256,768]{1,0:T(8,128)}, f32[256,768]{1,0:T(8,128)S(1)}, u32[]{:S(2)}) copy-start(f32[256,768]{1,0:T(8,128)S(1)} %get-tuple-element.111) | copy-start | bytes 2359300
  82.8 4.3 %copy-start.84 = (f32[256]{0:T(256)}, f32[256]{0:T(256)S(1)}, u32[]{:S(2)}) copy-start(f32[256]{0:T(256)S(1)} %get-tuple-element.104) | copy-start | bytes 3076
  82.8 4.3 %copy-start.86 = (f32[256]{0:T(256)}, f32[256]{0:T(256)S(1)}, u32[]{:S(2)}) copy-start(f32[256]{0:T(256)S(1)} %get-tuple-element.105) | copy-start | bytes 3076
  82.8 4.3 %copy-start.78 = (f32[256]{0:T(256)S(1)}, f32[256]{0:T(256)}, u32[]{:S(2)}) copy-start(f32[256]{0:T(256)} %copy-done.77) | copy-start | bytes 3076
  87.1 1.4 copy-start.19
  87.1 1.4 copy-start.21
  87.2 1.4 copy-start.23
  87.2 1.4 copy-start.25
  87.2 1.4 copy-start.27
  87.2 1.4 copy-start.29
  87.2 1.4 copy-start.31
  131.7 2.8 %copy-start.6 = (bf16[256,1536]{1,0:T(8,128)(2,1)S(1)}, bf16[256,1536]{1,0:T(8,128)(2,1)}, u32[]{:S(2)}) copy-start(bf16[256,1536]{1,0:T(8,128)(2,1)} %get-tuple-element.21) | copy-start | bytes 2359300
  134.5 2.6 %copy-start.82 = (f32[1,1536]{1,0:T(1,128)S(1)}, f32[1,1536]{1,0:T(1,128)}, u32[]{:S(2)}) copy-start(f32[1,1536]{1,0:T(1,128)} %get-tuple-element.22) | copy-start | bytes 18436
  134.5 3.8 %copy-start.2 = (f32[256,768]{1,0:T(8,128)S(1)}, f32[256,768]{1,0:T(8,128)}, u32[]{:S(2)}) copy-start(f32[256,768]{1,0:T(8,128)} %copy-done.1) | copy-start | bytes 2359300
  134.5 3.8 %copy-start.3 = (f32[16,16,768]{2,1,0:T(8,128)S(1)}, f32[16,16,768]{2,1,0:T(8,128)}, u32[]{:S(2)}) copy-start(f32[16,16,768]{2,1,0:T(8,128)} %get-tuple-element.103) | copy-start | bytes 2359300
  134.5 3.7 %copy-start.14 = (f32[768]{0:T(1024)S(1)}, f32[768]{0:T(1024)}, u32[]{:S(2)}) copy-start(f32[768]{0:T(1024)} %param.22) | copy-start | bytes 9220
  136.8 4.1 %copy-start.16 = (f32[768]{0:T(1024)S(1)}, f32[768]{0:T(1024)}, u32[]{:S(2)}) copy-start(f32[768]{0:T(1024)} %copy-done.15) | copy-start | bytes 9220
  136.8 4.1 %copy-start.18 = (f32[768]{0:T(1024)S(1)}, f32[768]{0:T(1024)}, u32[]{:S(2)}) copy-start(f32[768]{0:T(1024)} %copy-done.17) | copy-start | bytes 9220
  136.8 4.1 %copy-start.20 = (f32[768]{0:T(1024)S(1)}, f32[768]{0:T(1024)}, u32[]{:S(2)}) copy-start(f32[768]{0:T(1024)} %get-tuple-element.65) | copy-start | bytes 9220
  136.8 4.1 %copy-start.22 = (f32[768]{0:T(1024)S(1)}, f32[768]{0:T(1024)}, u32[]{:S(2)}) copy-start(f32[768]{0:T(1024)} %get-tuple-element.66) | copy-start | bytes 9220
  136.8 4.1 %copy-start.24 = (f32[768]{0:T(1024)S(1)}, f32[768]{0:T(1024)}, u32[]{:S(2)}) copy-start(f32[768]{0:T(1024)} %get-tuple-element.67) | copy-start | bytes 9220
  136.8 4.1 %copy-start.26 = (f32[768]{0:T(1024)S(1)}, f32[768]{0:T(1024)}, u32[]{:S(2)}) copy-start(f32[768]{0:T(1024)} %get-tuple-element.68) | copy-start | bytes 9220
  136.8 4.1 %copy-start.28 = (f32[768]{0:T(1024)S(1)}, f32[768]{0:T(1024)}, u32[]{:S(2)}) copy-start(f32[768]{0:T(1024)} %get-tuple-element.69) | copy-start | bytes 9220
  136.9 4.1 %copy-start.30 = (f32[768]{0:T(1024)S(1)}, f32[768]{0:T(1024)}, u32[]{:S(2)}) copy-start(f32[768]{0:T(1024)} %get-tuple-element.70) | copy-start | bytes 9220
  136.9 4.1 %copy-start.32 = (f32[768]{0:T(1024)S(1)}, f32[768]{0:T(1024)}, u32[]{:S(2)}) copy-start(f32[768]{0:T(1024)} %get-tuple-element.71) | copy-start | bytes 9220
  136.9 4.1 %copy-start.34 = (f32[768]{0:T(1024)S(1)}, f32[768]{0:T(1024)}, u32[]{:S(2)}) copy-start(f32[768]{0:T(1024)} %get-tuple-element.72) | copy-start | bytes 9220
  136.9 4.1 %copy-start.36 = (f32[768]{0:T(1024)S(1)}, f32[768]{0:T(1024)}, u32[]{:S(2)}) copy-start(f32[768]{0:T(1024)} %get-tuple-element.73) | copy-start | bytes 9220
  136.9 4.1 %copy-start.38 = (f32[768]{0:T(1024)S(1)}, f32[768]{0:T(1024)}, u32[]{:S(2)}) copy-start(f32[768]{0:T(1024)} %get-tuple-element.74) | copy-start | bytes 9220
  136.9 4.1 %copy-start.40 = (f32[768]{0:T(1024)S(1)}, f32[768]{0:T(1024)}, u32[]{:S(2)}) copy-start(f32[768]{0:T(1024)} %get-tuple-element.75) | copy-start | bytes 9220
  136.9 4.1 %copy-start.42 = (f32[768]{0:T(1024)S(1)}, f32[768]{0:T(1024)}, u32[]{:S(2)}) copy-start(f32[768]{0:T(1024)} %get-tuple-element.76) | copy-start | bytes 9220
  136.9 4.1 %copy-start.44 = (f32[768]{0:T(1024)S(1)}, f32[768]{0:T(1024)}, u32[]{:S(2)}) copy-start(f32[768]{0:T(1024)} %get-tuple-element.77) | copy-start | bytes 9220
  136.9 4.1 %copy-start.46 = (f32[768]{0:T(1024)S(1)}, f32[768]{0:T(1024)}, u32[]{:S(2)}) copy-start(f32[768]{0:T(1024)} %get-tuple-element.78) | copy-start | bytes 9220
  136.9 4.1 %copy-start.48 = (f32[768]{0:T(1024)S(1)}, f32[768]{0:T(1024)}, u32[]{:S(2)}) copy-start(f32[768]{0:T(1024)} %get-tuple-element.79) | copy-start | bytes 9220
  137.0 4.1 %copy-start.50 = (f32[768]{0:T(1024)S(1)}, f32[768]{0:T(1024)}, u32[]{:S(2)}) copy-start(f32[768]{0:T(1024)} %get-tuple-element.80) | copy-start | bytes 9220
  137.0 4.1 %copy-start.52 = (f32[768]{0:T(1024)S(1)}, f32[768]{0:T(1024)}, u32[]{:S(2)}) copy-start(f32[768]{0:T(1024)} %get-tuple-element.81) | copy-start | bytes 9220
  137.0 4.1 %copy-start.54 = (f32[768]{0:T(1024)S(1)}, f32[768]{0:T(1024)}, u32[]{:S(2)}) copy-start(f32[768]{0:T(1024)} %get-tuple-element.82) | copy-start | bytes 9220
  137.0 4.1 %copy-start.56 = (f32[768]{0:T(1024)S(1)}, f32[768]{0:T(1024)}, u32[]{:S(2)}) copy-start(f32[768]{0:T(1024)} %get-tuple-element.83) | copy-start | bytes 9220
  137.0 4.1 %copy-start.58 = (f32[768]{0:T(1024)S(1)}, f32[768]{0:T(1024)}, u32[]{:S(2)}) copy-start(f32[768]{0:T(1024)} %get-tuple-element.84) | copy-start | bytes 9220
  137.0 4.1 %copy-start.60 = (f32[768]{0:T(1024)S(1)}, f32[768]{0:T(1024)}, u32[]{:S(2)}) copy-start(f32[768]{0:T(1024)} %get-tuple-element.85) | copy-start | bytes 9220
  137.0 4.1 %copy-start.62 = (f32[768]{0:T(1024)S(1)}, f32[768]{0:T(1024)}, u32[]{:S(2)}) copy-start(f32[768]{0:T(1024)} %get-tuple-element.86) | copy-start | bytes 9220
  137.0 4.1 %copy-start.64 = (f32[768]{0:T(1024)S(1)}, f32[768]{0:T(1024)}, u32[]{:S(2)}) copy-start(f32[768]{0:T(1024)} %get-tuple-element.87) | copy-start | bytes 9220
  137.0 4.1 %copy-start.66 = (f32[768]{0:T(1024)S(1)}, f32[768]{0:T(1024)}, u32[]{:S(2)}) copy-start(f32[768]{0:T(1024)} %get-tuple-element.88) | copy-start | bytes 9220
  137.0 4.1 %copy-start.68 = (f32[768]{0:T(1024)S(1)}, f32[768]{0:T(1024)}, u32[]{:S(2)}) copy-start(f32[768]{0:T(1024)} %get-tuple-element.89) | copy-start | bytes 9220
  137.1 4.1 %copy-start.70 = (f32[768]{0:T(1024)S(1)}, f32[768]{0:T(1024)}, u32[]{:S(2)}) copy-start(f32[768]{0:T(1024)} %get-tuple-element.90) | copy-start | bytes 9220
  137.1 4.1 %copy-start.72 = (f32[768]{0:T(1024)S(1)}, f32[768]{0:T(1024)}, u32[]{:S(2)}) copy-start(f32[768]{0:T(1024)} %get-tuple-element.91) | copy-start | bytes 9220
  137.1 4.1 %copy-start.74 = (f32[768]{0:T(1024)S(1)}, f32[768]{0:T(1024)}, u32[]{:S(2)}) copy-start(f32[768]{0:T(1024)} %get-tuple-element.92) | copy-start | bytes 9220
  137.1 4.1 %copy-start.76 = (f32[768]{0:T(1024)S(1)}, f32[768]{0:T(1024)}, u32[]{:S(2)}) copy-start(f32[768]{0:T(1024)} %get-tuple-element.93) | copy-start | bytes 9220
  138.3 5.5 %copy-start.80 = (f32[768]{0:T(1024)}, f32[768]{0:T(1024)S(1)}, u32[]{:S(2)}) copy-start(f32[768]{0:T(1024)S(1)} %get-tuple-element.126) | copy-start | bytes 9220
  138.3 5.5 %copy-start.79 = (f32[256]{0:T(256)S(1)}, f32[256]{0:T(256)}, u32[]{:S(2)}) copy-start(f32[256]{0:T(256)} %copy-done.77) | copy-start | bytes 3076
  141.2 4.2 %copy-start.5 = (bf16[448,768]{1,0:T(8,128)(2,1)S(1)}, bf16[448,768]{1,0:T(8,128)(2,1)}, u32[]{:S(2)}) copy-start(bf16[448,768]{1,0:T(8,128)(2,1)} %copy-done.4) | copy-start | bytes 2064388
  146.6 1.6 copy-start.81
  146.6 1.7 copy-start.85
  146.6 1.7 copy-start.87
  (25 other events, 33.3 us)
